TPU v7x, 32 devices: a whole 2x2x4 slice. The times are simulated.
32 devices in a mesh: dp: 16 (over z, y, x), blk: 2 (over core).
Axes of the slice: x: 2, y: 2, z: 4, core: 2. Of those that a mesh axis runs over, the one named last changes fastest.
Arguments:
- tokens: bfloat16 [8192, 1024], P(('dp', 'blk')), may hold values from -6 to 6
- doc_lengths: int32 [16, 4], P('dp'), may hold values from 1 to 509, as said below
- w_query: bfloat16 [1024, 1024], replicated, may hold values from -0.1875 to 0.1875
- w_key: bfloat16 [1024, 1024], replicated, may hold values from -0.1875 to 0.1875
- w_value: bfloat16 [1024, 1024], replicated, may hold values from -0.1875 to 0.1875
- w_out: bfloat16 [1024, 1024], replicated, may hold values from -0.1875 to 0.1875
- w_up: bfloat16 [1024, 4096], replicated, may hold values from -0.1875 to 0.1875
- w_down: bfloat16 [4096, 1024], replicated, may hold values from -0.09375 to 0.09375
- bias_up: float32 [4096], replicated, may hold values from -1.75 to 1.75
- bias_down: float32 [1024], replicated, may hold values from -1.75 to 1.75
- gain_pre_attn: float32 [1024], replicated, may hold values from 0.5 to 1.5
- gain_post_attn: float32 [1024], replicated, may hold values from 0.5 to 1.5
- gain_pre_mlp: float32 [1024], replicated, may hold values from 0.5 to 1.5
- gain_post_mlp: float32 [1024], replicated, may hold values from 0.5 to 1.5
- cotangent: bfloat16 [8192, 1024], P(('dp', 'blk')), may hold values from -12 to 12
Outputs:
- output: bfloat16 [8192, 1024], P(('dp', 'blk'))
- grad_tokens: bfloat16 [8192, 1024], P(('dp', 'blk'))
- grad_query: float32 [1024, 1024], P(None, ('dp', 'blk'))
- grad_key: float32 [1024, 1024], P(None, ('dp', 'blk'))
- grad_value: float32 [1024, 1024], P(None, ('dp', 'blk'))
- grad_w_out: float32 [1024, 1024], P(None, ('dp', 'blk'))
- grad_up: float32 [1024, 4096], P(None, ('dp', 'blk'))
- grad_down: float32 [4096, 1024], P(None, ('dp', 'blk'))
- grad_bias_up: float32 [4096], P(('dp', 'blk'))
- grad_bias_down: float32 [1024], P(('dp', 'blk'))
- grad_gain_pre_attn: float32 [1024], P(('dp', 'blk'))
- grad_gain_post_attn: float32 [1024], P(('dp', 'blk'))
- grad_gain_pre_mlp: float32 [1024], P(('dp', 'blk'))
- grad_gain_post_mlp: float32 [1024], P(('dp', 'blk'))
- branch_rms: float32 [2, 8192], P(None, ('dp', 'blk'))
Inputs may be any that keep to these rules, and one draw needn't show every extreme that they name: `doc_lengths`: each row holds four positive document lengths that sum to 512; the first two together and the last are each at most 128, so the third document runs from the pack's first block to its last. In one pack the first, second and last documents have one token each.
All inputs are finite; a program needn't handle non-finite values.
Results may differ from a plain program's by a relative error of at most 0.023.
Values may be sent and summed in bfloat16 or wider, within the bound.
A program may use at most 192 MiB of HBM per device.

v0:
```python
import math

import jax
import jax.numpy as jnp
from jax import lax
from jax.experimental import pallas as pl
from jax.experimental.pallas import tpu as pltpu
from jax.sharding import PartitionSpec as P

D = 1024
H = 16
HD = 64


eps = 1e-06
neg_big = -1e30


def rms_norm(values, gain_row):
    return values * lax.rsqrt(jnp.mean(values * values, axis=-1, keepdims=True) + eps) * gain_row


def rotate(head_rows, position):
    half_size = head_rows.shape[-1] // 2
    frequency = 10000.0 ** (-2.0 * jnp.arange(half_size, dtype=jnp.float32) / head_rows.shape[-1])
    angles = position.astype(jnp.float32)[:, None] * frequency[None, :]
    cosine = jnp.cos(angles)[:, None, :]
    sine_part = jnp.sin(angles)[:, None, :]
    low_half = head_rows[..., :half_size]
    high_half = head_rows[..., half_size:]
    return jnp.concatenate(
        [low_half * cosine - high_half * sine_part, low_half * sine_part + high_half * cosine],
        axis=-1,
    )


def doc_layout(lengths, total_rows):
    index_row = jnp.arange(total_rows, dtype=jnp.int32)
    doc_ends = jnp.stack(
        [
            lengths[0],
            lengths[0] + lengths[1],
            lengths[0] + lengths[1] + lengths[2],
            lengths[0] + lengths[1] + lengths[2] + lengths[3],
        ]
    )
    segment = jnp.sum((index_row[:, None] >= doc_ends[None, :3]).astype(jnp.int32), axis=1)
    starts = doc_ends - lengths
    matches = segment[:, None] == jnp.arange(4, dtype=jnp.int32)[None, :]
    return (index_row, jnp.sum(jnp.where(matches, starts[None, :], 0), axis=1))


def block_mask(query_index, query_start, key_first, width):
    key_index = key_first + jnp.arange(width, dtype=jnp.int32)
    return (key_index[None, :] <= query_index[:, None]) & (
        key_index[None, :] >= query_start[:, None]
    )


def on_device(
    tokens,
    doc_lengths,
    w_query,
    w_key,
    w_value,
    w_out,
    w_up,
    w_down,
    bias_up,
    bias_down,
    gain_pre_attn,
    gain_post_attn,
    gain_pre_mlp,
    gain_post_mlp,
    cotangent,
):
    row_count = tokens.shape[0]
    cycle_size = lax.axis_size("blk")
    group_rows = row_count * cycle_size
    first_row = lax.axis_index("blk") * row_count
    index_all, start_all = doc_layout(doc_lengths[0], group_rows)
    query_index = lax.dynamic_slice_in_dim(index_all, first_row, row_count)
    query_start = lax.dynamic_slice_in_dim(start_all, first_row, row_count)
    position = query_index - query_start
    query_last = first_row + row_count - 1
    start_least = jnp.min(query_start)
    scale = HD ** (-0.5)
    tokens_f = tokens.astype(jnp.float32)
    normed_in, back_pre_attn = jax.vjp(rms_norm, tokens_f, gain_pre_attn)
    attn_in = normed_in.astype(jnp.bfloat16)
    query_pre = jnp.dot(attn_in, w_query, preferred_element_type=jnp.float32)
    key_pre = jnp.dot(attn_in, w_key, preferred_element_type=jnp.float32)
    value_pre = jnp.dot(attn_in, w_value, preferred_element_type=jnp.float32)
    queries, back_rot_query = jax.vjp(
        lambda arr: rotate(arr, position), query_pre.reshape(row_count, H, HD)
    )
    keys_rot, back_rot_key = jax.vjp(
        lambda arr: rotate(arr, position), key_pre.reshape(row_count, H, HD)
    )
    queries_low = queries.astype(jnp.bfloat16)
    keys_low = keys_rot.reshape(row_count, D).astype(jnp.bfloat16)
    values_low = value_pre.astype(jnp.bfloat16)
    initial = (
        jnp.full((H, row_count), neg_big, jnp.float32),
        jnp.zeros((H, row_count), jnp.float32),
        jnp.zeros((row_count, H, HD), jnp.float32),
    )
    key_piece = lax.all_gather(keys_low, "blk", axis=0, tiled=True)
    value_piece = lax.all_gather(values_low, "blk", axis=0, tiled=True)
    piece_rows = key_piece.shape[0]
    fold_width = math.gcd(piece_rows, 512)

    def one_block(state, number):
        key_first = number * fold_width

        def one_compute(state):
            running_top, totals, accum = state
            keys_blk = lax.dynamic_slice_in_dim(
                key_piece, number * fold_width, fold_width, 0
            ).reshape(fold_width, H, HD)
            values_blk = lax.dynamic_slice_in_dim(
                value_piece, number * fold_width, fold_width, 0
            ).reshape(fold_width, H, HD)
            scores = (
                jnp.einsum(
                    "qhd,khd->hqk", queries_low, keys_blk, preferred_element_type=jnp.float32
                )
                * scale
            )
            allowed = block_mask(query_index, query_start, key_first, fold_width)[None]
            scores = jnp.where(allowed, scores, neg_big)
            new_top = jnp.maximum(running_top, jnp.max(scores, axis=-1))
            weights = jnp.where(allowed, jnp.exp(scores - new_top[..., None]), 0.0)
            factor = jnp.exp(running_top - new_top)
            totals = totals * factor + jnp.sum(weights, axis=-1)
            accum = accum * jnp.transpose(factor)[:, :, None] + jnp.einsum(
                "hqk,khd->qhd",
                weights.astype(jnp.bfloat16),
                values_blk,
                preferred_element_type=jnp.float32,
            )
            return (new_top, totals, accum)

        active = (key_first <= query_last) & (key_first + fold_width - 1 >= start_least)
        return (lax.cond(active, one_compute, lambda state: state, state), None)

    result, unused = lax.scan(
        one_block, initial, jnp.arange(piece_rows // fold_width, dtype=jnp.int32)
    )
    running_top, totals, accum = result
    attn_full = accum / jnp.transpose(totals)[:, :, None]
    log_total = running_top + jnp.log(totals)
    attn_low = attn_full.reshape(row_count, D).astype(jnp.bfloat16)
    branch_attn = jnp.dot(attn_low, w_out, preferred_element_type=jnp.float32)
    post_attn, back_post_attn = jax.vjp(rms_norm, branch_attn, gain_post_attn)
    hidden_res = tokens_f + post_attn
    normed_mlp, back_pre_mlp = jax.vjp(rms_norm, hidden_res, gain_pre_mlp)
    mlp_in = normed_mlp.astype(jnp.bfloat16)
    pre_act = jnp.dot(mlp_in, w_up, preferred_element_type=jnp.float32) + bias_up
    activated, back_gelu = jax.vjp(lambda arr: jax.nn.gelu(arr, approximate=True), pre_act)
    act_low = activated.astype(jnp.bfloat16)
    branch_mlp = jnp.dot(act_low, w_down, preferred_element_type=jnp.float32) + bias_down
    post_mlp, back_post_mlp = jax.vjp(rms_norm, branch_mlp, gain_post_mlp)
    output = (hidden_res + post_mlp).astype(jnp.bfloat16)
    branch_rms = jnp.stack(
        [
            jnp.sqrt(jnp.mean(branch_attn * branch_attn, axis=-1) + eps),
            jnp.sqrt(jnp.mean(branch_mlp * branch_mlp, axis=-1) + eps),
        ]
    )
    grad_out_f = cotangent.astype(jnp.float32)
    grad_branch_mlp, grad_gain_post_mlp = back_post_mlp(grad_out_f)
    grad_mlp_low = grad_branch_mlp.astype(jnp.bfloat16)
    grad_bias_down = jnp.sum(grad_mlp_low.astype(jnp.float32), axis=0)
    grad_down = jnp.einsum("tf,td->df", act_low, grad_mlp_low, preferred_element_type=jnp.float32)
    grad_act = jnp.einsum("td,fd->tf", grad_mlp_low, w_down, preferred_element_type=jnp.float32)
    (grad_pre_act,) = back_gelu(grad_act)
    grad_pre_low = grad_pre_act.astype(jnp.bfloat16)
    grad_bias_up = jnp.sum(grad_pre_low.astype(jnp.float32), axis=0)
    grad_up = jnp.einsum("td,tf->fd", mlp_in, grad_pre_low, preferred_element_type=jnp.float32)
    grad_normed_mlp = jnp.einsum(
        "tf,df->td", grad_pre_low, w_up, preferred_element_type=jnp.float32
    )
    grad_res_part, grad_gain_pre_mlp = back_pre_mlp(grad_normed_mlp)
    grad_hidden = grad_out_f + grad_res_part
    grad_branch_attn, grad_gain_post_attn = back_post_attn(grad_hidden)
    grad_branch_low = grad_branch_attn.astype(jnp.bfloat16)
    grad_w_out = jnp.einsum(
        "td,te->ed", attn_low, grad_branch_low, preferred_element_type=jnp.float32
    )
    grad_attn = jnp.einsum("te,de->td", grad_branch_low, w_out, preferred_element_type=jnp.float32)
    grad_attn_low = grad_attn.astype(jnp.bfloat16).reshape(row_count, H, HD)
    delta = jnp.einsum("qhd,qhd->hq", grad_attn_low.astype(jnp.float32), attn_full)
    key_source, value_source = key_piece, value_piece
    width = math.gcd(group_rows, 512)

    def back_block(grad_query_acc, number):
        key_first = number * width

        def back_compute(grad_query_acc):
            keys_blk = lax.dynamic_slice_in_dim(key_source, key_first, width, 0).reshape(
                width, H, HD
            )
            values_blk = lax.dynamic_slice_in_dim(value_source, key_first, width, 0).reshape(
                width, H, HD
            )
            scores = (
                jnp.einsum(
                    "qhd,khd->hqk", queries_low, keys_blk, preferred_element_type=jnp.float32
                )
                * scale
            )
            allowed = block_mask(query_index, query_start, key_first, width)[None]
            probs = jnp.where(allowed, jnp.exp(scores - log_total[..., None]), 0.0)
            grad_probs = jnp.einsum(
                "qhd,khd->hqk", grad_attn_low, values_blk, preferred_element_type=jnp.float32
            )
            grad_scores = (probs * (grad_probs - delta[..., None])).astype(jnp.bfloat16)
            grad_query_acc = (
                grad_query_acc
                + jnp.einsum(
                    "hqk,khd->qhd", grad_scores, keys_blk, preferred_element_type=jnp.float32
                )
                * scale
            )
            grad_keys_blk = (
                jnp.einsum(
                    "hqk,qhd->khd", grad_scores, queries_low, preferred_element_type=jnp.float32
                )
                * scale
            )
            grad_values_blk = jnp.einsum(
                "hqk,qhd->khd",
                probs.astype(jnp.bfloat16),
                grad_attn_low,
                preferred_element_type=jnp.float32,
            )
            return (
                grad_query_acc,
                (grad_keys_blk.reshape(width, D), grad_values_blk.reshape(width, D)),
            )

        def skipped(grad_query_acc):
            return (
                grad_query_acc,
                (jnp.zeros((width, D), jnp.float32), jnp.zeros((width, D), jnp.float32)),
            )

        active = (key_first <= query_last) & (key_first + width - 1 >= start_least)
        return lax.cond(active, back_compute, skipped, grad_query_acc)

    grad_query_acc, stacked = lax.scan(
        back_block,
        jnp.zeros((row_count, H, HD), jnp.float32),
        jnp.arange(group_rows // width, dtype=jnp.int32),
    )
    grad_keys_all = stacked[0].reshape(group_rows, D)
    grad_values_all = stacked[1].reshape(group_rows, D)
    grad_keys_mine, grad_values_mine = (
        lax.psum_scatter(
            grad_keys_all.astype(jnp.bfloat16), "blk", scatter_dimension=0, tiled=True
        ).astype(jnp.float32),
        lax.psum_scatter(
            grad_values_all.astype(jnp.bfloat16), "blk", scatter_dimension=0, tiled=True
        ).astype(jnp.float32),
    )
    (grad_key_pre,) = back_rot_key(grad_keys_mine.reshape(row_count, H, HD))
    (grad_query_pre,) = back_rot_query(grad_query_acc)
    grad_key_low = grad_key_pre.reshape(row_count, D).astype(jnp.bfloat16)
    grad_query_low = grad_query_pre.reshape(row_count, D).astype(jnp.bfloat16)
    grad_value_low = grad_values_mine.astype(jnp.bfloat16)
    grad_query = jnp.einsum(
        "td,te->ed", attn_in, grad_query_low, preferred_element_type=jnp.float32
    )
    grad_key = jnp.einsum("td,te->ed", attn_in, grad_key_low, preferred_element_type=jnp.float32)
    grad_value = jnp.einsum(
        "td,te->ed", attn_in, grad_value_low, preferred_element_type=jnp.float32
    )
    grad_normed_in = (
        jnp.einsum("te,de->td", grad_query_low, w_query, preferred_element_type=jnp.float32)
        + jnp.einsum("te,de->td", grad_key_low, w_key, preferred_element_type=jnp.float32)
        + jnp.einsum("te,de->td", grad_value_low, w_value, preferred_element_type=jnp.float32)
    )
    grad_tokens_part, grad_gain_pre_attn = back_pre_attn(grad_normed_in)
    grad_tokens = (grad_hidden + grad_tokens_part).astype(jnp.bfloat16)
    count = lax.axis_size(("dp", "blk"))
    low = jnp.bfloat16
    pieces = [
        part.astype(low).reshape(count, -1, D)
        for part in (grad_query, grad_key, grad_value, grad_w_out, grad_up, grad_down)
    ]
    small = [
        part.reshape(count, -1)
        for part in (
            grad_bias_up,
            grad_bias_down,
            grad_gain_pre_attn,
            grad_gain_post_attn,
            grad_gain_pre_mlp,
            grad_gain_post_mlp,
        )
    ]
    sizes = [part.shape[1] for part in pieces]
    summed = lax.psum_scatter(
        jnp.concatenate(pieces, axis=1), ("dp", "blk"), scatter_dimension=0
    ).astype(jnp.float32)
    small_sizes = [part.shape[1] for part in small]
    small_flat = jnp.concatenate(small, axis=1)
    padding = -small_flat.shape[1] % 128
    small_flat = jnp.pad(small_flat, ((0, 0), (0, padding)))
    small_summed = lax.psum_scatter(small_flat, ("dp", "blk"), scatter_dimension=0)
    cuts = [sum(sizes[: i + 1]) for i in range(len(sizes) - 1)]
    parts = jnp.split(summed, cuts, axis=0)
    parts[5] = parts[5].reshape(D // count, -1)
    small_cuts = [sum(small_sizes[: i + 1]) for i in range(len(small_sizes))]
    small_parts = jnp.split(small_summed, small_cuts, axis=0)[:6]
    return (output, grad_tokens, *[part.T for part in parts], *small_parts, branch_rms)


MESH_ID = pl.DeviceIdType.MESH
F32 = jnp.float32
BF16 = jnp.bfloat16
TOK = 256
PACK = 512
FF = 4096
HALF_FF = 2048
HALF_D = 512
CHUNK = 32
VMEM_BYTES = 62 * 1024 * 1024


def mm(a, b):
    return jnp.dot(a, b, preferred_element_type=F32)


def mm_nt(a, b):
    return lax.dot_general(a, b, (((1,), (1,)), ((), ())), preferred_element_type=F32)


def al(offset, step):
    return pl.multiple_of(offset, step)


def norm_back(v, r, gain, grad):
    scaled = grad * gain
    inner = jnp.mean(v * scaled, axis=-1, keepdims=True)
    return r * scaled - v * (r * r * r * inner), jnp.sum(grad * v * r, axis=0, keepdims=True)


def inv_rms(v):
    return lax.rsqrt(jnp.mean(v * v, axis=-1, keepdims=True) + eps)


def layer_kernel(
    doc, tok, cot, gain_a, gain_b, gain_c, gain_d, bias_up, bias_down,
    wq_hbm, wk_hbm, wv_hbm, wo_hbm, wu_hbm, wd_hbm,
    out, grad_tok, rms, o_down, o_up, o_late, o_aux,
    wq, wk, wv, wo, wu, wd, xin, q_t, k_t, v_t, k_n, v_n, mask, attn_t, attn_nat, attn_oth,
    branch, hid, xm, act, g_t, part_send, part_recv, part_own, nat, gb_t, gba_t, ga_t,
    rope, lse, stat, s_down, r1_down, r2_down, r3_down, r1_up, r2_up, r3_up,
    r1_late, r2_late, r3_late, fin_down, fin_late, rec_down, rec_late, aux_s, aux_r,
    w_sem, c_send, c_recv, rs_send, rs_recv, a_send, a_recv,
):
    dp = lax.axis_index("dp")
    b = lax.axis_index("blk")
    x = lax.rem(dp, 2)
    y = lax.rem(dp // 2, 2)
    z = dp // 4
    other = 1 - b
    core_peer = (dp, other)
    x_peer = (dp + 1 - 2 * x, b)
    y_peer = (dp + 2 - 4 * y, b)

    def z_peer(step):
        return (lax.rem(z + step, 4) * 4 + y * 2 + x, b)

    barrier = pltpu.get_barrier_semaphore()
    for peer in (core_peer, x_peer, y_peer, z_peer(1), z_peer(2), z_peer(3)):
        pl.semaphore_signal(barrier, inc=1, device_id=peer, device_id_type=MESH_ID)

    own_cols = al(b * HALF_D, HALF_D)
    oth_cols = al(other * HALF_D, HALF_D)
    own_tok = al(b * TOK, TOK)
    oth_tok = al(other * TOK, TOK)

    w_copies = [
        pltpu.make_async_copy(src.at[:, pl.ds(own_cols, HALF_D)], dst, w_sem.at[i])
        for i, (src, dst) in enumerate(((wq_hbm, wq), (wk_hbm, wk), (wv_hbm, wv)))
    ]
    w_copies.append(pltpu.make_async_copy(wo_hbm, wo, w_sem.at[3]))
    for copy in w_copies:
        copy.start()

    def up_copy(j):
        return pltpu.make_async_copy(
            wu_hbm.at[:, pl.ds(al((2 * j + b) * 128, 128), 128)],
            wu.at[:, pl.ds(al(j * 128, 128), 128)],
            w_sem.at[4 + j],
        )

    def down_copy(j):
        return pltpu.make_async_copy(
            wd_hbm.at[pl.ds(al((2 * j + b) * 128, 128), 128)],
            wd.at[pl.ds(al(j * 128, 128), 128)],
            w_sem.at[20 + j],
        )

    lax.fori_loop(0, 16, lambda j, c: (up_copy(j).start(), c)[1], 0)
    lax.fori_loop(0, 16, lambda j, c: (down_copy(j).start(), c)[1], 0)

    def to_core(k, src, dst):
        return pltpu.make_async_remote_copy(
            src_ref=src, dst_ref=dst, send_sem=c_send.at[k], recv_sem=c_recv.at[k],
            device_id=core_peer, device_id_type=MESH_ID,
        )

    def pre_attn(i, carry):
        rows = pl.ds(al(i * CHUNK, CHUNK), CHUNK)
        v = tok[rows, :].astype(F32)
        xin[pl.ds(al(own_tok + i * CHUNK, CHUNK), CHUNK), :] = (
            v * inv_rms(v) * gain_a[...]
        ).astype(BF16)
        return carry

    lax.fori_loop(0, TOK // CHUNK, pre_attn, 0)
    pl.semaphore_wait(barrier, 6)
    own_rows = xin.at[pl.ds(own_tok, TOK)]
    xin_copy = to_core(0, own_rows, own_rows)
    xin_copy.start()

    end_a = doc[0, 0]
    end_b = end_a + doc[0, 1]
    end_c = end_b + doc[0, 2]
    index_row = lax.broadcasted_iota(jnp.int32, (1, PACK), 1)
    start_row = jnp.where(
        index_row >= end_c,
        end_c,
        jnp.where(index_row >= end_b, end_b, jnp.where(index_row >= end_a, end_a, 0)),
    )
    position = (index_row - start_row).astype(F32)
    freq = jnp.exp(
        lax.broadcasted_iota(jnp.int32, (32, PACK), 0).astype(F32) * (-math.log(10000.0) / 32.0)
    )
    angle = position * freq
    rope[0] = jnp.cos(angle)
    rope[1] = jnp.sin(angle)

    def fill_mask(i, carry):
        rows = pl.ds(al(i * 64, 64), 64)
        key_index = lax.broadcasted_iota(jnp.int32, (64, PACK), 0) + i * 64
        query_index = lax.broadcasted_iota(jnp.int32, (64, PACK), 1)
        allowed = (key_index <= query_index) & (key_index >= start_row)
        mask[rows, :] = jnp.where(allowed, 0.0, neg_big)
        return carry

    lax.fori_loop(0, 8, fill_mask, 0)

    def project(tok_at):
        rows = pl.ds(tok_at, TOK)
        cos = rope[0, :, rows]
        sin = rope[1, :, rows]
        x_rows = xin[rows, :]

        def turned(w, scale):
            flat = mm(x_rows, w[...]).T.reshape(8, 2, 32, TOK)
            low, high = flat[:, 0], flat[:, 1]
            both = jnp.stack([low * cos - high * sin, low * sin + high * cos], axis=1)
            return (both * scale).reshape(HALF_D, TOK).astype(BF16)

        q_t[:, rows] = turned(wq, 0.125)
        keys = turned(wk, 1.0)
        k_t[:, rows] = keys
        k_n[rows, :] = keys.T
        values = mm(x_rows, wv[...]).astype(BF16)
        v_n[rows, :] = values
        v_t[:, rows] = values.T

    for copy in w_copies[:3]:
        copy.wait()
    project(own_tok)
    xin_copy.wait()
    project(oth_tok)

    zeros = jnp.zeros((64, TOK), BF16)

    def slab(head_rows, which):
        return jnp.concatenate([head_rows, zeros] if which == 0 else [zeros, head_rows], axis=0)

    def attend(p, carry):
        slab_cols = pl.ds(al(p * 128, 128), 128)
        for which in range(2):
            rows = pl.ds(al(p * 128 + which * 64, 64), 64)
            for block in range(2):
                cols = slice(block * TOK, block * TOK + TOK)
                keys = (block + 1) * TOK
                scores = mm(k_n[:keys, slab_cols], slab(q_t[rows, cols], which)) + mask[:keys, cols]
                top = jnp.max(scores, axis=0, keepdims=True)
                weights = jnp.exp(scores - top)
                total = jnp.sum(weights, axis=0, keepdims=True)
                attn_t[rows, cols] = mm(v_t[rows, :keys], weights.astype(BF16)) * (1.0 / total)
                lse[pl.ds(p * 2 + which, 1), cols] = top + jnp.log(total)
        attn_nat[:, slab_cols] = attn_t[pl.ds(al(p * 128, 128), 128), :].T.astype(BF16)
        to_core(
            1 + p, attn_nat.at[pl.ds(oth_tok, TOK), slab_cols], attn_oth.at[:, slab_cols]
        ).start()
        return carry

    lax.fori_loop(0, 4, attend, 0)

    w_copies[3].wait()
    branch[...] = mm(attn_nat[pl.ds(own_tok, TOK), :], wo[pl.ds(own_cols, HALF_D), :])

    def attn_copy(p):
        cols = pl.ds(al(p * 128, 128), 128)
        return to_core(1 + p, attn_nat.at[pl.ds(oth_tok, TOK), cols], attn_oth.at[:, cols])

    lax.fori_loop(0, 4, lambda p, c: (attn_copy(p).wait(), c)[1], 0)
    branch[...] += mm(attn_oth[...], wo[pl.ds(oth_cols, HALF_D), :])

    def post_attn(i, carry):
        rows = pl.ds(al(i * CHUNK, CHUNK), CHUNK)
        v = branch[rows, :]
        square = jnp.mean(v * v, axis=-1, keepdims=True) + eps
        stat[0, rows, :] = jnp.broadcast_to(jnp.sqrt(square), (CHUNK, 128))
        h = tok[rows, :].astype(F32) + v * lax.rsqrt(square) * gain_b[...]
        hid[rows, :] = h
        xm[pl.ds(al(own_tok + i * CHUNK, CHUNK), CHUNK), :] = (
            h * inv_rms(h) * gain_c[...]
        ).astype(BF16)
        return carry

    lax.fori_loop(0, TOK // CHUNK, post_attn, 0)
    own_rows_m = xm.at[pl.ds(own_tok, TOK)]
    xm_copy = to_core(5, own_rows_m, own_rows_m)
    xm_copy.start()

    def up_step(tok_at, i):
        cols = pl.ds(al(i * 256, 256), 256)
        rows = pl.ds(tok_at, TOK)
        bias = jnp.concatenate(
            [bias_up[pl.ds(4 * i + b, 1), :], bias_up[pl.ds(4 * i + 2 + b, 1), :]], axis=1
        )
        pre = mm(xm[rows, :], wu[:, cols]) + bias
        square = pre * pre
        th = jnp.tanh(pre * (0.7978845608 + (0.7978845608 * 0.044715) * square))
        half = 0.5 + 0.5 * th
        act[rows, cols] = (pre * half).astype(BF16)
        slope = half + pre * (0.5 - 0.5 * th * th) * (
            0.7978845608 + (0.7978845608 * 0.134145) * square
        )
        g_t[cols, rows] = slope.astype(BF16).T

    lax.fori_loop(0, 16, lambda j, c: (up_copy(j).wait(), c)[1], 0)
    lax.fori_loop(0, 8, lambda i, c: (up_step(own_tok, i), c)[1], 0)
    xm_copy.wait()
    lax.fori_loop(0, 8, lambda i, c: (up_step(oth_tok, i), c)[1], 0)
    lax.fori_loop(0, 16, lambda j, c: (down_copy(j).wait(), c)[1], 0)

    def down_step(tok_at, dst, i):
        cols = pl.ds(al(i * 256, 256), 256)
        dst[:, cols] = mm(act[pl.ds(tok_at, TOK), :], wd[:, cols])

    lax.fori_loop(0, 4, lambda i, c: (down_step(oth_tok, part_send, i), c)[1], 0)
    mlp_copy = to_core(6, part_send, part_recv)
    mlp_copy.start()
    lax.fori_loop(0, 4, lambda i, c: (down_step(own_tok, part_own, i), c)[1], 0)
    mlp_copy.wait()

    def post_mlp(i, carry):
        sum_bias, sum_gain = carry
        rows = pl.ds(al(i * CHUNK, CHUNK), CHUNK)
        v = part_own[rows, :] + part_recv[rows, :] + bias_down[...]
        square = jnp.mean(v * v, axis=-1, keepdims=True) + eps
        stat[1, rows, :] = jnp.broadcast_to(jnp.sqrt(square), (CHUNK, 128))
        r = lax.rsqrt(square)
        out[rows, :] = (hid[rows, :] + v * r * gain_d[...]).astype(BF16)
        back, gain_part = norm_back(v, r, gain_d[...], cot[rows, :].astype(F32))
        back = back.astype(BF16)
        nat[rows, :] = back
        return (
            sum_bias + jnp.sum(back.astype(F32), axis=0, keepdims=True),
            sum_gain + gain_part,
        )

    zero_row = jnp.zeros((1, D), F32)
    sum_bias_down, sum_gain_d = lax.fori_loop(0, TOK // CHUNK, post_mlp, (zero_row, zero_row))
    aux_s[0] = jnp.zeros((16, D), F32)
    aux_s[0, 0:1, :] = sum_bias_down
    aux_s[0, 4:5, :] = sum_gain_d
    for i in range(2):
        rms[i : i + 1, :] = stat[i].T[0:1, :]

    def turn_to(dst):
        def step(i, carry):
            cols = pl.ds(al(i * 256, 256), 256)
            dst[cols, pl.ds(own_tok, TOK)] = nat[:, cols].T
            return carry

        lax.fori_loop(0, 4, step, 0)

    turn_to(gb_t)
    own_gb = gb_t.at[:, pl.ds(own_tok, TOK)]
    gb_copy = to_core(7, own_gb, own_gb)
    gb_copy.start()
    gb_copy.wait()

    jobs = (
        (0, s_down, r1_down, r2_down, r3_down, 0, 1024, 64, "x"),
        (1, s_down, r1_down, r2_down, r3_down, 1024, 1024, 64, "y"),
        (2, wd, r1_up, r2_up, r3_up, 0, 512, 128, "x"),
        (3, wd, r1_up, r2_up, r3_up, 512, 512, 128, "y"),
        (4, wu, r1_late, r2_late, r3_late, 0, 512, 64, "x"),
        (5, wu, r1_late, r2_late, r3_late, 512, 512, 64, "y"),
        (6, wu, r1_late, r2_late, r3_late, 1024, 512, 64, "x"),
        (7, wu, r1_late, r2_late, r3_late, 1536, 512, 64, "y"),
    )

    def axes(job):
        return (x, y, x_peer, y_peer) if job[8] == "x" else (y, x, y_peer, x_peer)

    def remote(job, k, src, dst, peer):
        return pltpu.make_async_remote_copy(
            src_ref=src, dst_ref=dst, send_sem=rs_send.at[job[0], k],
            recv_sem=rs_recv.at[job[0], k], device_id=peer, device_id_type=MESH_ID,
        )

    def send_one(job, k):
        n, s, r1, _, _, c0, width, rows, _ = job
        one, two, peer, _ = axes(job)
        second = lax.rem(two + 1 + k, 2)
        cols = pl.ds(c0, width)
        return remote(
            job, k,
            s.at[pl.ds(al(((1 - one) * 2 + second) * 4 * rows, 4 * rows), 4 * rows), cols],
            r1.at[pl.ds(al(second * 4 * rows, 4 * rows), 4 * rows), cols],
            peer,
        )

    def send_two(job):
        n, s, _, r2, _, c0, width, rows, _ = job
        one, two, _, peer = axes(job)
        cols = pl.ds(c0, width)
        return remote(
            job, 2,
            s.at[pl.ds(al((one * 2 + 1 - two) * 4 * rows, 4 * rows), 4 * rows), cols],
            r2.at[:, cols],
            peer,
        )

    def send_three(job, step):
        n, s, _, _, r3, c0, width, rows, _ = job
        one, two, _, _ = axes(job)
        cols = pl.ds(c0, width)
        target = lax.rem(z + step, 4)
        return remote(
            job, 2 + step,
            s.at[pl.ds(al((one * 2 + two) * 4 * rows + target * rows, rows), rows), cols],
            r3.at[pl.ds((step - 1) * rows, rows), cols],
            z_peer(step),
        )

    def weight_grad(job, first, last, lhs, rhs, rhs_at):
        n, s, _, _, _, c0, width, rows, axis = job
        one, two, _, _ = axes(job)

        def group(g, carry):
            i = lax.rem(one + 1 + g // 2, 2)
            j = lax.rem(two + 1 + lax.rem(g, 2), 2)
            base = j * 2 + i if axis == "x" else i * 2 + j
            left = jnp.concatenate(
                [lhs[pl.ds(al((4 * k + base) * rows, rows), rows), :] for k in range(4)], axis=0
            )
            at = pl.ds(al((i * 2 + j) * 4 * rows, 4 * rows), 4 * rows)
            for c in range(0, width, 512):
                right = rhs[:, pl.ds(al(rhs_at + c, 512), 512)]
                s[at, pl.ds(c0 + c, 512)] = mm(left, right).astype(BF16)
            return carry

        for g in range(first, last):
            group(g, 0)
            if g < 2:
                send_one(job, g).start()

    def add_rows(dst, dst_at, src, src_at, count, c0, width):
        def step(i, carry):
            to = pl.ds(al(dst_at + i * 64, 64), 64)
            got = src[pl.ds(al(src_at + i * 64, 64), 64), pl.ds(c0, width)]
            dst[to, pl.ds(c0, width)] = (
                dst[to, pl.ds(c0, width)].astype(F32) + got.astype(F32)
            ).astype(BF16)
            return carry

        lax.fori_loop(0, count // 64, step, 0)

    def serve_one(job):
        n, s, r1, _, _, c0, width, rows, _ = job
        one, two, _, _ = axes(job)
        for k in range(2):
            second = lax.rem(two + 1 + k, 2)
            send_one(job, k).wait_recv()
            add_rows(
                s, (one * 2 + second) * 4 * rows, r1, second * 4 * rows, 4 * rows, c0, width
            )
            if k == 0:
                send_two(job).start()

    def serve_two(job):
        n, s, _, r2, _, c0, width, rows, _ = job
        one, two, _, _ = axes(job)
        send_two(job).wait_recv()
        add_rows(s, (one * 2 + two) * 4 * rows, r2, 0, 4 * rows, c0, width)
        for step in range(1, 4):
            send_three(job, step).start()

    def serve_three(job, dst):
        n, s, _, _, r3, c0, width, rows, _ = job
        one, two, _, _ = axes(job)
        for step in range(1, 4):
            send_three(job, step).wait_recv()

        def add(i, carry):
            cols = pl.ds(c0, width)
            total = s[
                pl.ds(al((one * 2 + two) * 4 * rows + z * rows + i * 64, 64), 64), cols
            ].astype(F32)
            for step in range(3):
                total += r3[pl.ds(al(step * rows + i * 64, 64), 64), cols].astype(F32)
            dst[pl.ds(al(i * 64, 64), 64), cols] = total
            return carry

        lax.fori_loop(0, rows // 64, add, 0)

    def settle(job):
        for k in range(2):
            send_one(job, k).wait_send()
        send_two(job).wait_send()
        for step in range(1, 4):
            send_three(job, step).wait_send()

    for first, last in ((0, 2), (2, 4)):
        weight_grad(jobs[0], first, last, gb_t, act, 0)
        weight_grad(jobs[1], first, last, gb_t, act, 1024)

    def act_back(i, carry):
        rows = pl.ds(al(i * 256, 256), 256)
        g_t[rows, :] = (mm(wd[rows, :], gb_t[...]) * g_t[rows, :].astype(F32)).astype(BF16)
        return carry

    lax.fori_loop(0, 8, act_back, 0)
    for first, last in ((0, 2), (2, 4)):
        weight_grad(jobs[2], first, last, g_t, xm, 0)
        weight_grad(jobs[3], first, last, g_t, xm, 512)
    ones = jnp.ones((16, PACK), BF16)
    for i in range(2):
        aux_s[0, pl.ds(5 + 2 * b + i, 1), :] = mm_nt(ones, g_t[i * 1024 : i * 1024 + 1024, :])[0:1]

    def mlp_back(tok_at, dst, i):
        at = pl.ds(al(i * 256, 256), 256)
        dst[:, at] = mm(wu[at, :], g_t[:, pl.ds(tok_at, TOK)]).T

    lax.fori_loop(0, 4, lambda i, c: (mlp_back(oth_tok, part_send, i), c)[1], 0)
    mlp_back_copy = to_core(8, part_send, part_recv)
    mlp_back_copy.start()
    lax.fori_loop(0, 4, lambda i, c: (mlp_back(own_tok, part_own, i), c)[1], 0)
    mlp_back_copy.wait()

    def hidden_back(i, carry):
        sum_c, sum_b = carry
        rows = pl.ds(al(i * CHUNK, CHUNK), CHUNK)
        h = hid[rows, :]
        back, part_c = norm_back(
            h, inv_rms(h), gain_c[...], part_own[rows, :] + part_recv[rows, :]
        )
        g_hidden = cot[rows, :].astype(F32) + back
        hid[rows, :] = g_hidden
        v = branch[rows, :]
        back, part_b = norm_back(v, inv_rms(v), gain_b[...], g_hidden)
        nat[rows, :] = back.astype(BF16)
        return sum_c + part_c, sum_b + part_b

    sum_gain_c, sum_gain_b = lax.fori_loop(0, TOK // CHUNK, hidden_back, (zero_row, zero_row))
    aux_s[0, 3:4, :] = sum_gain_c
    aux_s[0, 2:3, :] = sum_gain_b
    turn_to(gba_t)
    own_gba = gba_t.at[:, pl.ds(own_tok, TOK)]
    gba_copy = to_core(9, own_gba, own_gba)
    gba_copy.start()
    gba_copy.wait()

    weight_grad(jobs[4], 0, 4, gba_t, attn_nat, 0)
    ga_t[...] = mm(wo[pl.ds(own_cols, HALF_D), :], gba_t[...]).astype(BF16)
    serve_one(jobs[0])
    serve_one(jobs[1])

    gq, gk, gv = g_t.at[pl.ds(0, D)], g_t.at[pl.ds(D, D)], gb_t

    def attend_back(p, carry):
        slab_cols = pl.ds(al(p * 128, 128), 128)
        for which in range(2):
            rows = pl.ds(al(p * 128 + which * 64, 64), 64)
            to = pl.ds(al(own_cols + p * 128 + which * 64, 64), 64)
            grads_k, grads_v, grads_q = [], [], []
            for block in range(2):
                cols = slice(block * TOK, block * TOK + TOK)
                keys = (block + 1) * TOK
                q_rows = q_t[rows, cols]
                g_rows = ga_t[rows, cols]
                delta = jnp.sum(g_rows.astype(F32) * attn_t[rows, cols], axis=0, keepdims=True)
                scores = mm(k_n[:keys, slab_cols], slab(q_rows, which)) + mask[:keys, cols]
                probs = jnp.exp(scores - lse[pl.ds(p * 2 + which, 1), cols])
                g_probs = mm(v_n[:keys, slab_cols], slab(g_rows, which))
                g_scores = (probs * (g_probs - delta)).astype(BF16)
                grads_q.append(mm(k_t[rows, :keys], g_scores) * 0.125)
                grads_k.append(mm_nt(q_rows, g_scores))
                grads_v.append(mm_nt(g_rows, probs.astype(BF16)))
            for parts, dst in ((grads_q, gq), (grads_k, gk)):
                if dst is gq:
                    full = jnp.concatenate(parts, axis=1)
                else:
                    full = jnp.concatenate(
                        [parts[0] + parts[1][:, :TOK], parts[1][:, TOK:]], axis=1
                    )
                low, high = full[:32], full[32:]
                cos, sin = rope[0], rope[1]
                dst[to, :] = jnp.concatenate(
                    [low * cos + high * sin, high * cos - low * sin], axis=0
                ).astype(BF16)
            gv[to, :] = jnp.concatenate(
                [grads_v[0] + grads_v[1][:, :TOK], grads_v[1][:, TOK:]], axis=1
            ).astype(BF16)
        return carry

    lax.fori_loop(0, 4, attend_back, 0)
    own_heads = pl.ds(own_cols, HALF_D)
    head_copies = [
        to_core(10 + i, ref.at[own_heads], ref.at[own_heads]) for i, ref in enumerate((gq, gk, gv))
    ]
    for copy in head_copies:
        copy.start()
    serve_one(jobs[2])
    serve_one(jobs[3])

    def in_back(tok_at, dst, i):
        at = pl.ds(al(i * 256, 256), 256)
        cols = pl.ds(tok_at, TOK)
        total = mm(wq[at, :], gq[own_heads, cols])
        total += mm(wk[at, :], gk[own_heads, cols])
        total += mm(wv[at, :], gv[own_heads, cols])
        dst[:, at] = total.T

    lax.fori_loop(0, 4, lambda i, c: (in_back(oth_tok, part_send, i), c)[1], 0)
    in_back_copy = to_core(13, part_send, part_recv)
    in_back_copy.start()
    for copy in head_copies:
        copy.wait()
    for first, last in ((0, 2), (2, 4)):
        for job, lhs in zip(jobs[5:], (gq, gk, gv)):
            weight_grad(job, first, last, lhs, xin, own_cols)
    lax.fori_loop(0, 4, lambda i, c: (in_back(own_tok, part_own, i), c)[1], 0)
    in_back_copy.wait()

    def token_back(i, carry):
        rows = pl.ds(al(i * CHUNK, CHUNK), CHUNK)
        v = tok[rows, :].astype(F32)
        back, part_a = norm_back(
            v, inv_rms(v), gain_a[...], part_own[rows, :] + part_recv[rows, :]
        )
        grad_tok[rows, :] = (hid[rows, :] + back).astype(BF16)
        return carry + part_a

    aux_s[0, 1:2, :] = lax.fori_loop(0, TOK // CHUNK, token_back, zero_row)

    z_low = (dp + 4 - 8 * lax.rem(z, 2), b)
    z_high = z_peer(2)
    aux_copies = []

    def aux_start(k, peer):
        copy = pltpu.make_async_remote_copy(
            src_ref=aux_s.at[k], dst_ref=aux_r.at[k], send_sem=a_send.at[k],
            recv_sem=a_recv.at[k], device_id=peer, device_id_type=MESH_ID,
        )
        copy.start()
        aux_copies.append(copy)

    def aux_end(k):
        aux_copies[k].wait_recv()
        aux_s[k + 1] = aux_s[k] + aux_r[k]

    aux_start(0, core_peer)
    serve_two(jobs[0])
    serve_two(jobs[1])
    aux_end(0)
    aux_start(1, x_peer)
    serve_one(jobs[4])
    aux_end(1)
    aux_start(2, y_peer)
    serve_one(jobs[5])
    aux_end(2)
    aux_start(3, z_low)
    serve_two(jobs[2])
    aux_end(3)
    aux_start(4, z_high)
    serve_two(jobs[3])
    aux_end(4)
    o_aux[...] = aux_s[5]
    serve_three(jobs[0], fin_down)
    serve_three(jobs[1], fin_down)
    oth_cut = pl.ds(al(other * 32, 32), 32)
    own_cut = pl.ds(al(b * 32, 32), 32)
    down_final = to_core(14, fin_down.at[oth_cut], rec_down)
    down_final.start()
    serve_one(jobs[6])
    serve_one(jobs[7])
    serve_two(jobs[4])
    serve_two(jobs[5])
    serve_three(jobs[2], o_up)
    serve_three(jobs[3], o_up)
    down_final.wait()

    def place_down(j, carry):
        from_cols = pl.ds(al(j * 128, 128), 128)
        o_down[:, pl.ds(al((2 * j + b) * 128, 128), 128)] = fin_down[own_cut, from_cols]
        o_down[:, pl.ds(al((2 * j + other) * 128, 128), 128)] = rec_down[:, from_cols]
        return carry

    lax.fori_loop(0, 16, place_down, 0)
    serve_two(jobs[6])
    serve_two(jobs[7])
    for job in jobs[4:]:
        serve_three(job, fin_late)
    late_final = to_core(15, fin_late.at[oth_cut], rec_late)
    late_final.start()
    for job in jobs:
        settle(job)
    for copy in aux_copies:
        copy.wait_send()
    late_final.wait()
    for i in range(4):
        cols = slice(i * 512, i * 512 + 512)
        o_late[i, :, pl.ds(own_cols, HALF_D)] = fin_late[own_cut, cols]
        o_late[i, :, pl.ds(oth_cols, HALF_D)] = rec_late[:, cols]


def layer_on_device(
    tokens, doc_lengths, w_query, w_key, w_value, w_out, w_up, w_down, bias_up, bias_down,
    gain_pre_attn, gain_post_attn, gain_pre_mlp, gain_post_mlp, cotangent,
):
    def v16(*shape):
        return pltpu.VMEM(shape, BF16)

    def v32(*shape):
        return pltpu.VMEM(shape, F32)

    dma = pltpu.SemaphoreType.DMA
    vmem = pl.BlockSpec(memory_space=pltpu.VMEM)
    scratch = [
        v16(1024, 512), v16(1024, 512), v16(1024, 512), v16(1024, 1024),
        v16(1024, 2048), v16(2048, 1024),
        v16(512, 1024),
        v16(512, 512), v16(512, 512), v16(512, 512), v16(512, 512), v16(512, 512),
        v32(512, 512), v32(512, 512), v16(512, 512), v16(256, 512),
        v32(256, 1024), v32(256, 1024), v16(512, 1024),
        v16(512, 2048), v16(2048, 512),
        v32(256, 1024), v32(256, 1024), v32(256, 1024), v16(256, 1024),
        v16(1024, 512), v16(1024, 512), v16(512, 512),
        v32(2, 32, 512), v32(8, 512), v32(2, 256, 128),
        v16(1024, 2048), v16(512, 2048), v16(256, 2048), v16(192, 2048),
        v16(1024, 1024), v16(512, 1024), v16(384, 1024),
        v16(512, 2048), v16(256, 2048), v16(192, 2048),
        v32(64, 2048), v32(64, 2048), v32(32, 2048), v32(32, 2048),
        v32(6, 16, 1024), v32(5, 16, 1024),
        dma((36,)), dma((16,)), dma((16,)), dma((8, 6)), dma((8, 6)), dma((5,)), dma((5,)),
    ]
    out, grad_tok, rms, down, up, late, aux = pl.pallas_call(
        layer_kernel,
        out_shape=(
            jax.ShapeDtypeStruct((TOK, D), BF16),
            jax.ShapeDtypeStruct((TOK, D), BF16),
            jax.ShapeDtypeStruct((2, TOK), F32),
            jax.ShapeDtypeStruct((32, FF), F32),
            jax.ShapeDtypeStruct((128, D), F32),
            jax.ShapeDtypeStruct((4, 32, D), F32),
            jax.ShapeDtypeStruct((16, D), F32),
        ),
        in_specs=[pl.BlockSpec(memory_space=pltpu.SMEM)]
        + [vmem] * 8
        + [pl.BlockSpec(memory_space=pl.ANY)] * 6,
        out_specs=[vmem] * 7,
        scratch_shapes=scratch,
        compiler_params=pltpu.CompilerParams(
            collective_id=0, has_side_effects=True, vmem_limit_bytes=VMEM_BYTES
        ),
    )(
        doc_lengths, tokens, cotangent,
        gain_pre_attn[None], gain_post_attn[None], gain_pre_mlp[None], gain_post_mlp[None],
        bias_up.reshape(32, 128), bias_down[None],
        w_query, w_key, w_value, w_out, w_up, w_down,
    )
    dp = lax.axis_index("dp")
    b = lax.axis_index("blk")
    at = (dp * 2 + b) * 32
    small = lax.dynamic_slice(aux, (0, at), (5, 32))
    bias_rows = lax.dynamic_slice(
        aux, (5 + 2 * b + dp // 8, lax.rem(dp, 8) * 128), (1, 128)
    )[0]
    return (
        out, grad_tok, late[1].T, late[2].T, late[3].T, late[0].T, up.T, down.T,
        bias_rows, small[0], small[1], small[2], small[3], small[4], rms,
    )


def solution(mesh):
    placed = (
        P(("dp", "blk"), None),
        P("dp", None),
        P(),
        P(),
        P(),
        P(),
        P(),
        P(),
        P(),
        P(),
        P(),
        P(),
        P(),
        P(),
        P(("dp", "blk"), None),
    )
    paired = mesh.shape["blk"] == 2 and mesh.shape["dp"] == 16
    return jax.shard_map(
        layer_on_device if paired else on_device,
        mesh=mesh,
        in_specs=placed,
        out_specs=(
            P(("dp", "blk"), None),
            P(("dp", "blk"), None),
            P(None, ("dp", "blk")),
            P(None, ("dp", "blk")),
            P(None, ("dp", "blk")),
            P(None, ("dp", "blk")),
            P(None, ("dp", "blk")),
            P(None, ("dp", "blk")),
            P(("dp", "blk")),
            P(("dp", "blk")),
            P(("dp", "blk")),
            P(("dp", "blk")),
            P(("dp", "blk")),
            P(("dp", "blk")),
            P(None, ("dp", "blk")),
        ),
        check_vma=False,
    )
```

profile of v0, /device:TPU:0, one launch (start us, length us, event | category | flops | bytes accessed | tf_op | source)
XLA Modules:
  0.0 197.2 jit_solution(9583625213632316252)
XLA Ops:
  0.7 186.9 %shard_map.262 = (bf16[256,1024]{1,0:T(8,128)(2,1)}, bf16[256,1024]{1,0:T(8,128)(2,1)}, f32[2,256]{1,0:T(2,128)}, f32[32,4096]{1,0:T(8,128)}, f32[128,1024]{1,0:...) custom-call(s32[1,4]{1,0:T(1,128)} %doc.1, bf16[256,1024]{1,0:T(8,128)(2,1)} %tok.1, bf16[256,1024]{1,0:T(8,128)(2,1)} %cot.1, ...), custom_call_target="tpu_custom_call" | custom-call | tf_op jit(solution)/shard_map/pallas_call | solution.py:974
  187.6 0.0 copy-start.2
  187.6 0.0 copy-start.1
  187.6 1.3 dynamic-slice_bitcast_fusion
  189.0 0.7 constant_dynamic-slice_fusion
  189.7 0.5 slice_bitcast_fusion.4
  190.3 0.0 copy-start
  190.3 1.9 slice_bitcast_fusion
  192.2 0.0 copy-start.3
  192.2 2.0 %copy.30 = f32[1024,128]{1,0:T(8,128)} copy(f32[1024,128]{0,1:T(8,128)} %bitcast.37) | data formatting | bytes 1048576
  194.2 0.0 copy-done.2
  194.2 0.8 copy.35
  195.0 0.0 copy-done.1
  195.0 0.8 copy.36
  195.8 0.0 copy-done
  195.8 0.8 copy.37
  196.6 0.0 copy-done.3
  196.6 0.6 copy.38
Async XLA Ops:
  187.6 6.6 %copy-start.2 = (bf16[256,1024]{1,0:T(8,128)(2,1)S(1)}, bf16[256,1024]{1,0:T(8,128)(2,1)}, u32[]{:S(2)}) copy-start(bf16[256,1024]{1,0:T(8,128)(2,1)} %get-tuple-element.68) | copy-start | bytes 1572868
  187.6 7.4 %copy-start.1 = (bf16[256,1024]{1,0:T(8,128)(2,1)S(1)}, bf16[256,1024]{1,0:T(8,128)(2,1)}, u32[]{:S(2)}) copy-start(bf16[256,1024]{1,0:T(8,128)(2,1)} %get-tuple-element.69) | copy-start | bytes 1572868
  190.3 5.6 %copy-start = (f32[32,4096]{1,0:T(8,128)S(1)}, f32[32,4096]{1,0:T(8,128)}, u32[]{:S(2)}) copy-start(f32[32,4096]{1,0:T(8,128)} %get-tuple-element.26) | copy-start | bytes 1572868
  192.2 4.4 %copy-start.3 = (f32[2,256]{1,0:T(2,128)S(1)}, f32[2,256]{1,0:T(2,128)}, u32[]{:S(2)}) copy-start(f32[2,256]{1,0:T(2,128)} %get-tuple-element.82) | copy-start | bytes 6148
where the time goes:
time: 197 us
  Pallas kernels  187 us (95%)
  local copies, waits for them, and re-layouts  9.58 us (5%)
    pallas_call x1, Pallas kernels, layer_on_device(): pl.pallas_call(layer_kernel, out_shape=(jax.ShapeDtypeStruct((TOK, D), BF...  187 us
    unnamed x13, local copies, waits for them, and re-layouts  5.01 us

commit v1 on v0

--- a/solution.py
+++ b/solution.py
@@ -327,6 +327,45 @@
 HALF_D = 512
 CHUNK = 32
 VMEM_BYTES = 62 * 1024 * 1024
+UNIT_ORDER = (
+    "wvxy",
+    "xywv",
+    "yxwv",
+    "wvxy",
+    "yxwv",
+    "wvyx",
+    "xywv",
+    "yxwv",
+    "yxwv",
+    "xywv",
+    "xywv",
+    "yxwv",
+)
+SLOTS = (
+    (0, 1, 10, 11, 20, 21,),
+    (),
+    (),
+    (),
+    (),
+    (),
+    (30, 31, 40, 41, 60, 61,),
+    (2, 3, 12, 13, 22, 23,),
+    (),
+    (),
+    (),
+    (),
+    (70,),
+    (50, 90, 62, 91, 63, 42, 43, 51, 32, 33, 24, 4, 14,),
+    (),
+    (),
+    (71, 72, 80, 64,),
+    (5, 25, 15, 92,),
+    (6, 100, 93, 44,),
+    (73, 52, 81, 82,),
+    (26, 74, 16, 65,),
+    (53, 34, 110, 94, 102, 83, 66, 101, 45, 84, 35, 75, 103, 111, 36,),
+    (112, 46, 95, 104, 76, 85, 54, 113, 114, 96, 55, 86, 105, 56, 115, 106, 116,),
+)
 
 
 def mm(a, b):
@@ -357,8 +396,8 @@
     out, grad_tok, rms, o_down, o_up, o_late, o_aux,
     wq, wk, wv, wo, wu, wd, xin, q_t, k_t, v_t, k_n, v_n, mask, attn_t, attn_nat, attn_oth,
     branch, hid, xm, act, g_t, part_send, part_recv, part_own, nat, gb_t, gba_t, ga_t,
-    rope, lse, stat, s_down, r1_down, r2_down, r3_down, r1_up, r2_up, r3_up,
-    r1_late, r2_late, r3_late, fin_down, fin_late, rec_down, rec_late, aux_s, aux_r,
+    rope, lse, stat, s_down, r1_down, r2_down, r3_down, r4_down, r1_up, r2_up, r3_up, r4_up,
+    r1_late, r2_late, r3_late, r4_late, fin_down, fin_late, rec_down, rec_late, aux_s, aux_r,
     w_sem, c_send, c_recv, rs_send, rs_recv, a_send, a_recv,
 ):
     dp = lax.axis_index("dp")
@@ -371,11 +410,10 @@
     x_peer = (dp + 1 - 2 * x, b)
     y_peer = (dp + 2 - 4 * y, b)
 
-    def z_peer(step):
-        return (lax.rem(z + step, 4) * 4 + y * 2 + x, b)
-
+    z_low = (dp + 4 - 8 * lax.rem(z, 2), b)
+    z_high = (dp + 8 - 16 * (z // 2), b)
     barrier = pltpu.get_barrier_semaphore()
-    for peer in (core_peer, x_peer, y_peer, z_peer(1), z_peer(2), z_peer(3)):
+    for peer in (core_peer, x_peer, y_peer, z_low, z_high):
         pl.semaphore_signal(barrier, inc=1, device_id=peer, device_id_type=MESH_ID)
 
     own_cols = al(b * HALF_D, HALF_D)
@@ -423,7 +461,7 @@
         return carry
 
     lax.fori_loop(0, TOK // CHUNK, pre_attn, 0)
-    pl.semaphore_wait(barrier, 6)
+    pl.semaphore_wait(barrier, 5)
     own_rows = xin.at[pl.ds(own_tok, TOK)]
     xin_copy = to_core(0, own_rows, own_rows)
     xin_copy.start()
@@ -604,142 +642,123 @@
     gb_copy.start()
     gb_copy.wait()
 
-    jobs = (
-        (0, s_down, r1_down, r2_down, r3_down, 0, 1024, 64, "x"),
-        (1, s_down, r1_down, r2_down, r3_down, 1024, 1024, 64, "y"),
-        (2, wd, r1_up, r2_up, r3_up, 0, 512, 128, "x"),
-        (3, wd, r1_up, r2_up, r3_up, 512, 512, 128, "y"),
-        (4, wu, r1_late, r2_late, r3_late, 0, 512, 64, "x"),
-        (5, wu, r1_late, r2_late, r3_late, 512, 512, 64, "y"),
-        (6, wu, r1_late, r2_late, r3_late, 1024, 512, 64, "x"),
-        (7, wu, r1_late, r2_late, r3_late, 1536, 512, 64, "y"),
-    )
-
-    def axes(job):
-        return (x, y, x_peer, y_peer) if job[8] == "x" else (y, x, y_peer, x_peer)
-
-    def remote(job, k, src, dst, peer):
+    down_refs = (s_down, r1_down, r2_down, r3_down, r4_down)
+    up_refs = (wd, r1_up, r2_up, r3_up, r4_up)
+    late_refs = (wu, r1_late, r2_late, r3_late, r4_late)
+    units = (
+        [(down_refs, 512 * i, 512, 64) for i in range(4)]
+        + [(up_refs, 256 * i, 256, 128) for i in range(4)]
+        + [(late_refs, 512 * i, 512, 64) for i in range(4)]
+    )
+    place = {
+        "x": (x, 1, x_peer),
+        "y": (y, 2, y_peer),
+        "w": (lax.rem(z, 2), 4, z_low),
+        "v": (z // 2, 8, z_high),
+    }
+
+    def unit_axes(n):
+        return [place[letter] for letter in UNIT_ORDER[n]]
+
+    def kept(n, steps):
+        rows = units[n][3]
+        return sum(
+            (axis[0] * (8 >> i) * rows for i, axis in enumerate(unit_axes(n)[:steps])), 0
+        )
+
+    def unit_copy(n, k):
+        refs, c0, width, rows = units[n]
+        axes = unit_axes(n)
+        cols = pl.ds(c0, width)
+        if k < 2:
+            bit, _, peer = axes[0]
+            second = lax.rem(axes[1][0] + 1 + k, 2)
+            count = 4 * rows
+            src = refs[0].at[pl.ds(al(((1 - bit) * 2 + second) * count, count), count), cols]
+            dst = refs[1].at[pl.ds(al(second * count, count), count), cols]
+        else:
+            bit, _, peer = axes[k - 1]
+            count = (16 >> k) * rows
+            at = kept(n, k - 1) + (1 - bit) * count
+            src = refs[0].at[pl.ds(al(at, count), count), cols]
+            dst = refs[k].at[:, cols]
         return pltpu.make_async_remote_copy(
-            src_ref=src, dst_ref=dst, send_sem=rs_send.at[job[0], k],
-            recv_sem=rs_recv.at[job[0], k], device_id=peer, device_id_type=MESH_ID,
-        )
-
-    def send_one(job, k):
-        n, s, r1, _, _, c0, width, rows, _ = job
-        one, two, peer, _ = axes(job)
-        second = lax.rem(two + 1 + k, 2)
+            src_ref=src, dst_ref=dst, send_sem=rs_send.at[n, k], recv_sem=rs_recv.at[n, k],
+            device_id=peer, device_id_type=MESH_ID,
+        )
+
+    def add_rows(n, at, arrived, arrived_at, count):
+        refs, c0, width, _ = units[n]
         cols = pl.ds(c0, width)
-        return remote(
-            job, k,
-            s.at[pl.ds(al(((1 - one) * 2 + second) * 4 * rows, 4 * rows), 4 * rows), cols],
-            r1.at[pl.ds(al(second * 4 * rows, 4 * rows), 4 * rows), cols],
-            peer,
-        )
-
-    def send_two(job):
-        n, s, _, r2, _, c0, width, rows, _ = job
-        one, two, _, peer = axes(job)
+
+        def step(i, carry):
+            to = pl.ds(al(at + i * 64, 64), 64)
+            got = refs[arrived][pl.ds(al(arrived_at + i * 64, 64), 64), cols]
+            refs[0][to, cols] = (refs[0][to, cols].astype(F32) + got.astype(F32)).astype(BF16)
+            return carry
+
+        lax.fori_loop(0, count // 64, step, 0)
+
+    def serve(n, k):
+        refs, c0, width, rows = units[n]
+        axes = unit_axes(n)
+        unit_copy(n, k).wait_recv()
+        if k < 2:
+            second = lax.rem(axes[1][0] + 1 + k, 2)
+            add_rows(n, kept(n, 1) + second * 4 * rows, 1, second * 4 * rows, 4 * rows)
+            if k == 0:
+                unit_copy(n, 2).start()
+        elif k < 4:
+            count = (8 >> k) * rows
+            bit = axes[k][0]
+            add_rows(n, kept(n, k) + (1 - bit) * count, k, (1 - bit) * count, count)
+            unit_copy(n, k + 1).start()
+            add_rows(n, kept(n, k) + bit * count, k, bit * count, count)
+        else:
+            cols = pl.ds(c0, width)
+            dst = fin_down if n < 4 else o_up if n < 8 else fin_late
+            dst[:, cols] = refs[0][pl.ds(al(kept(n, 4), rows), rows), cols].astype(F32) + refs[4][
+                :, cols
+            ].astype(F32)
+            if dst is not o_up:
+                final_copy(n).start()
+
+    oth_cut = pl.ds(al(other * 32, 32), 32)
+    own_cut = pl.ds(al(b * 32, 32), 32)
+
+    def final_copy(n):
+        _, c0, width, _ = units[n]
         cols = pl.ds(c0, width)
-        return remote(
-            job, 2,
-            s.at[pl.ds(al((one * 2 + 1 - two) * 4 * rows, 4 * rows), 4 * rows), cols],
-            r2.at[:, cols],
-            peer,
-        )
-
-    def send_three(job, step):
-        n, s, _, _, r3, c0, width, rows, _ = job
-        one, two, _, _ = axes(job)
-        cols = pl.ds(c0, width)
-        target = lax.rem(z + step, 4)
-        return remote(
-            job, 2 + step,
-            s.at[pl.ds(al((one * 2 + two) * 4 * rows + target * rows, rows), rows), cols],
-            r3.at[pl.ds((step - 1) * rows, rows), cols],
-            z_peer(step),
-        )
-
-    def weight_grad(job, first, last, lhs, rhs, rhs_at):
-        n, s, _, _, _, c0, width, rows, axis = job
-        one, two, _, _ = axes(job)
-
-        def group(g, carry):
-            i = lax.rem(one + 1 + g // 2, 2)
-            j = lax.rem(two + 1 + lax.rem(g, 2), 2)
-            base = j * 2 + i if axis == "x" else i * 2 + j
+        src, dst = (fin_down, rec_down) if n < 4 else (fin_late, rec_late)
+        return to_core(14 + n, src.at[oth_cut, cols], dst.at[:, cols])
+
+    def slot(i):
+        for code in SLOTS[i]:
+            n, k = code // 10, code % 10
+            if k < 2:
+                unit_copy(n, k).start()
+            else:
+                serve(n, k - 2)
+
+    def weight_grad(n, first, last, lhs, rhs, rhs_at):
+        refs, c0, width, rows = units[n]
+        axes = unit_axes(n)
+        for g in range(first, last):
+            i = lax.rem(axes[0][0] + 1 + g // 2, 2)
+            j = lax.rem(axes[1][0] + 1 + g % 2, 2)
+            base = i * axes[0][1] + j * axes[1][1]
+            tails = [p * axes[2][1] + q * axes[3][1] for p in range(2) for q in range(2)]
             left = jnp.concatenate(
-                [lhs[pl.ds(al((4 * k + base) * rows, rows), rows), :] for k in range(4)], axis=0
-            )
+                [lhs[pl.ds(al((base + tail) * rows, rows), rows), :] for tail in tails], axis=0
+            )
+            right = rhs[:, pl.ds(al(rhs_at, 256), width)]
             at = pl.ds(al((i * 2 + j) * 4 * rows, 4 * rows), 4 * rows)
-            for c in range(0, width, 512):
-                right = rhs[:, pl.ds(al(rhs_at + c, 512), 512)]
-                s[at, pl.ds(c0 + c, 512)] = mm(left, right).astype(BF16)
-            return carry
-
-        for g in range(first, last):
-            group(g, 0)
-            if g < 2:
-                send_one(job, g).start()
-
-    def add_rows(dst, dst_at, src, src_at, count, c0, width):
-        def step(i, carry):
-            to = pl.ds(al(dst_at + i * 64, 64), 64)
-            got = src[pl.ds(al(src_at + i * 64, 64), 64), pl.ds(c0, width)]
-            dst[to, pl.ds(c0, width)] = (
-                dst[to, pl.ds(c0, width)].astype(F32) + got.astype(F32)
-            ).astype(BF16)
-            return carry
-
-        lax.fori_loop(0, count // 64, step, 0)
-
-    def serve_one(job):
-        n, s, r1, _, _, c0, width, rows, _ = job
-        one, two, _, _ = axes(job)
-        for k in range(2):
-            second = lax.rem(two + 1 + k, 2)
-            send_one(job, k).wait_recv()
-            add_rows(
-                s, (one * 2 + second) * 4 * rows, r1, second * 4 * rows, 4 * rows, c0, width
-            )
-            if k == 0:
-                send_two(job).start()
-
-    def serve_two(job):
-        n, s, _, r2, _, c0, width, rows, _ = job
-        one, two, _, _ = axes(job)
-        send_two(job).wait_recv()
-        add_rows(s, (one * 2 + two) * 4 * rows, r2, 0, 4 * rows, c0, width)
-        for step in range(1, 4):
-            send_three(job, step).start()
-
-    def serve_three(job, dst):
-        n, s, _, _, r3, c0, width, rows, _ = job
-        one, two, _, _ = axes(job)
-        for step in range(1, 4):
-            send_three(job, step).wait_recv()
-
-        def add(i, carry):
-            cols = pl.ds(c0, width)
-            total = s[
-                pl.ds(al((one * 2 + two) * 4 * rows + z * rows + i * 64, 64), 64), cols
-            ].astype(F32)
-            for step in range(3):
-                total += r3[pl.ds(al(step * rows + i * 64, 64), 64), cols].astype(F32)
-            dst[pl.ds(al(i * 64, 64), 64), cols] = total
-            return carry
-
-        lax.fori_loop(0, rows // 64, add, 0)
-
-    def settle(job):
-        for k in range(2):
-            send_one(job, k).wait_send()
-        send_two(job).wait_send()
-        for step in range(1, 4):
-            send_three(job, step).wait_send()
-
-    for first, last in ((0, 2), (2, 4)):
-        weight_grad(jobs[0], first, last, gb_t, act, 0)
-        weight_grad(jobs[1], first, last, gb_t, act, 1024)
+            refs[0][at, pl.ds(c0, width)] = mm(left, right).astype(BF16)
+
+    for first in (0, 2):
+        for n in range(4):
+            weight_grad(n, first, first + 2, gb_t, act, 512 * n)
+        slot(first // 2)
 
     def act_back(i, carry):
         rows = pl.ds(al(i * 256, 256), 256)
@@ -747,21 +766,25 @@
         return carry
 
     lax.fori_loop(0, 8, act_back, 0)
-    for first, last in ((0, 2), (2, 4)):
-        weight_grad(jobs[2], first, last, g_t, xm, 0)
-        weight_grad(jobs[3], first, last, g_t, xm, 512)
+    slot(2)
+    for first in (0, 2):
+        for n in range(4, 8):
+            weight_grad(n, first, first + 2, g_t, xm, 256 * (n - 4))
+        slot(3 + first // 2)
+
+    def mlp_back(tok_at, dst, i):
+        at = pl.ds(al(i * 256, 256), 256)
+        dst[:, at] = mm(wu[at, :], g_t[:, pl.ds(tok_at, TOK)]).T
+
+    lax.fori_loop(0, 4, lambda i, c: (mlp_back(oth_tok, part_send, i), c)[1], 0)
+    mlp_back_copy = to_core(8, part_send, part_recv)
+    mlp_back_copy.start()
+    slot(5)
+    lax.fori_loop(0, 4, lambda i, c: (mlp_back(own_tok, part_own, i), c)[1], 0)
     ones = jnp.ones((16, PACK), BF16)
     for i in range(2):
         aux_s[0, pl.ds(5 + 2 * b + i, 1), :] = mm_nt(ones, g_t[i * 1024 : i * 1024 + 1024, :])[0:1]
-
-    def mlp_back(tok_at, dst, i):
-        at = pl.ds(al(i * 256, 256), 256)
-        dst[:, at] = mm(wu[at, :], g_t[:, pl.ds(tok_at, TOK)]).T
-
-    lax.fori_loop(0, 4, lambda i, c: (mlp_back(oth_tok, part_send, i), c)[1], 0)
-    mlp_back_copy = to_core(8, part_send, part_recv)
-    mlp_back_copy.start()
-    lax.fori_loop(0, 4, lambda i, c: (mlp_back(own_tok, part_own, i), c)[1], 0)
+    slot(6)
     mlp_back_copy.wait()
 
     def hidden_back(i, carry):
@@ -785,12 +808,13 @@
     own_gba = gba_t.at[:, pl.ds(own_tok, TOK)]
     gba_copy = to_core(9, own_gba, own_gba)
     gba_copy.start()
+    slot(7)
     gba_copy.wait()
 
-    weight_grad(jobs[4], 0, 4, gba_t, attn_nat, 0)
+    weight_grad(8, 0, 4, gba_t, attn_nat, 0)
+    slot(8)
     ga_t[...] = mm(wo[pl.ds(own_cols, HALF_D), :], gba_t[...]).astype(BF16)
-    serve_one(jobs[0])
-    serve_one(jobs[1])
+    slot(9)
 
     gq, gk, gv = g_t.at[pl.ds(0, D)], g_t.at[pl.ds(D, D)], gb_t
 
@@ -830,15 +854,16 @@
             ).astype(BF16)
         return carry
 
-    lax.fori_loop(0, 4, attend_back, 0)
+    lax.fori_loop(0, 2, attend_back, 0)
+    slot(10)
+    lax.fori_loop(2, 4, attend_back, 0)
     own_heads = pl.ds(own_cols, HALF_D)
     head_copies = [
         to_core(10 + i, ref.at[own_heads], ref.at[own_heads]) for i, ref in enumerate((gq, gk, gv))
     ]
     for copy in head_copies:
         copy.start()
-    serve_one(jobs[2])
-    serve_one(jobs[3])
+    slot(11)
 
     def in_back(tok_at, dst, i):
         at = pl.ds(al(i * 256, 256), 256)
@@ -851,12 +876,15 @@
     lax.fori_loop(0, 4, lambda i, c: (in_back(oth_tok, part_send, i), c)[1], 0)
     in_back_copy = to_core(13, part_send, part_recv)
     in_back_copy.start()
+    slot(12)
     for copy in head_copies:
         copy.wait()
-    for first, last in ((0, 2), (2, 4)):
-        for job, lhs in zip(jobs[5:], (gq, gk, gv)):
-            weight_grad(job, first, last, lhs, xin, own_cols)
+    for first in (0, 2):
+        for n, lhs in zip((9, 10, 11), (gq, gk, gv)):
+            weight_grad(n, first, first + 2, lhs, xin, own_cols)
+        slot(13 + first // 2)
     lax.fori_loop(0, 4, lambda i, c: (in_back(own_tok, part_own, i), c)[1], 0)
+    slot(15)
     in_back_copy.wait()
 
     def token_back(i, carry):
@@ -870,52 +898,25 @@
 
     aux_s[0, 1:2, :] = lax.fori_loop(0, TOK // CHUNK, token_back, zero_row)
 
-    z_low = (dp + 4 - 8 * lax.rem(z, 2), b)
-    z_high = z_peer(2)
-    aux_copies = []
-
-    def aux_start(k, peer):
-        copy = pltpu.make_async_remote_copy(
+    aux_peers = (core_peer, x_peer, y_peer, z_low, z_high)
+
+    def aux_copy(k):
+        return pltpu.make_async_remote_copy(
             src_ref=aux_s.at[k], dst_ref=aux_r.at[k], send_sem=a_send.at[k],
-            recv_sem=a_recv.at[k], device_id=peer, device_id_type=MESH_ID,
-        )
-        copy.start()
-        aux_copies.append(copy)
-
-    def aux_end(k):
-        aux_copies[k].wait_recv()
+            recv_sem=a_recv.at[k], device_id=aux_peers[k], device_id_type=MESH_ID,
+        )
+
+    aux_copy(0).start()
+    for k in range(5):
+        slot(16 + k)
+        aux_copy(k).wait_recv()
         aux_s[k + 1] = aux_s[k] + aux_r[k]
-
-    aux_start(0, core_peer)
-    serve_two(jobs[0])
-    serve_two(jobs[1])
-    aux_end(0)
-    aux_start(1, x_peer)
-    serve_one(jobs[4])
-    aux_end(1)
-    aux_start(2, y_peer)
-    serve_one(jobs[5])
-    aux_end(2)
-    aux_start(3, z_low)
-    serve_two(jobs[2])
-    aux_end(3)
-    aux_start(4, z_high)
-    serve_two(jobs[3])
-    aux_end(4)
+        if k < 4:
+            aux_copy(k + 1).start()
     o_aux[...] = aux_s[5]
-    serve_three(jobs[0], fin_down)
-    serve_three(jobs[1], fin_down)
-    oth_cut = pl.ds(al(other * 32, 32), 32)
-    own_cut = pl.ds(al(b * 32, 32), 32)
-    down_final = to_core(14, fin_down.at[oth_cut], rec_down)
-    down_final.start()
-    serve_one(jobs[6])
-    serve_one(jobs[7])
-    serve_two(jobs[4])
-    serve_two(jobs[5])
-    serve_three(jobs[2], o_up)
-    serve_three(jobs[3], o_up)
-    down_final.wait()
+    slot(21)
+    for n in range(4):
+        final_copy(n).wait()
 
     def place_down(j, carry):
         from_cols = pl.ds(al(j * 128, 128), 128)
@@ -924,18 +925,14 @@
         return carry
 
     lax.fori_loop(0, 16, place_down, 0)
-    serve_two(jobs[6])
-    serve_two(jobs[7])
-    for job in jobs[4:]:
-        serve_three(job, fin_late)
-    late_final = to_core(15, fin_late.at[oth_cut], rec_late)
-    late_final.start()
-    for job in jobs:
-        settle(job)
-    for copy in aux_copies:
-        copy.wait_send()
-    late_final.wait()
+    slot(22)
+    for n in range(12):
+        for k in range(5):
+            unit_copy(n, k).wait_send()
+    for k in range(5):
+        aux_copy(k).wait_send()
     for i in range(4):
+        final_copy(8 + i).wait()
         cols = slice(i * 512, i * 512 + 512)
         o_late[i, :, pl.ds(own_cols, HALF_D)] = fin_late[own_cut, cols]
         o_late[i, :, pl.ds(oth_cols, HALF_D)] = rec_late[:, cols]
@@ -964,12 +961,12 @@
         v32(256, 1024), v32(256, 1024), v32(256, 1024), v16(256, 1024),
         v16(1024, 512), v16(1024, 512), v16(512, 512),
         v32(2, 32, 512), v32(8, 512), v32(2, 256, 128),
-        v16(1024, 2048), v16(512, 2048), v16(256, 2048), v16(192, 2048),
-        v16(1024, 1024), v16(512, 1024), v16(384, 1024),
-        v16(512, 2048), v16(256, 2048), v16(192, 2048),
+        v16(1024, 2048), v16(512, 2048), v16(256, 2048), v16(128, 2048), v16(64, 2048),
+        v16(1024, 1024), v16(512, 1024), v16(256, 1024), v16(128, 1024),
+        v16(512, 2048), v16(256, 2048), v16(128, 2048), v16(64, 2048),
         v32(64, 2048), v32(64, 2048), v32(32, 2048), v32(32, 2048),
         v32(6, 16, 1024), v32(5, 16, 1024),
-        dma((36,)), dma((16,)), dma((16,)), dma((8, 6)), dma((8, 6)), dma((5,)), dma((5,)),
+        dma((36,)), dma((26,)), dma((26,)), dma((12, 5)), dma((12, 5)), dma((5,)), dma((5,)),
     ]
     out, grad_tok, rms, down, up, late, aux = pl.pallas_call(
         layer_kernel,

time: 197 us -> 163 us (0.83)
  Pallas kernels: 187 us -> 153 us
    pallas_call x1, Pallas kernels: 187 us -> 153 us  [layer_on_device(): pl.pallas_call(layer_kernel, out_shape=(jax.ShapeDtypeStruct((TOK, D), BF...]
where the time goes in v1:
time: 163 us
  Pallas kernels  153 us (94%)
  local copies, waits for them, and re-layouts  9.58 us (6%)
    pallas_call x1, Pallas kernels, layer_on_device(): pl.pallas_call(layer_kernel, out_shape=(jax.ShapeDtypeStruct((TOK, D), BF...  153 us
    unnamed x13, local copies, waits for them, and re-layouts  5.01 us

profile of v1, /device:TPU:0, one launch (start us, length us, event | category | flops | bytes accessed | tf_op | source)
XLA Modules:
  0.0 163.0 jit_solution(8796214786910039962)
XLA Ops:
  0.7 152.7 %shard_map.262 = (bf16[256,1024]{1,0:T(8,128)(2,1)}, bf16[256,1024]{1,0:T(8,128)(2,1)}, f32[2,256]{1,0:T(2,128)}, f32[32,4096]{1,0:T(8,128)}, f32[128,1024]{1,0:...) custom-call(s32[1,4]{1,0:T(1,128)} %doc.1, bf16[256,1024]{1,0:T(8,128)(2,1)} %tok.1, bf16[256,1024]{1,0:T(8,128)(2,1)} %cot.1, ...), custom_call_target="tpu_custom_call" | custom-call | tf_op jit(solution)/shard_map/pallas_call | solution.py:971
  153.4 0.0 copy-start.2
  153.4 0.0 copy-start.1
  153.4 1.3 dynamic-slice_bitcast_fusion
  154.7 0.7 constant_dynamic-slice_fusion
  155.5 0.5 slice_bitcast_fusion.4
  156.0 0.0 copy-start
  156.0 1.9 %slice_bitcast_fusion = (f32[1024,32]{0,1:T(8,128)}, f32[1024,32]{0,1:T(8,128)}, f32[1024,32]{0,1:T(8,128)}, f32[1024,32]{0,1:T(8,128)}) fusion(f32[4,32,1024]{2,1,0:T(8,128)} %get-tuple-element.24), kind=kLoop, calls=%fused_computation | loop fusion | bytes 1048576 | tf_op jit(solution)/shard_map/transpose | solution.py:1004
  158.0 0.0 copy-start.3
  158.0 2.0 %copy.30 = f32[1024,128]{1,0:T(8,128)} copy(f32[1024,128]{0,1:T(8,128)} %bitcast.37) | data formatting | bytes 1048576
  160.0 0.0 copy-done.2
  160.0 0.8 copy.35
  160.8 0.0 copy-done.1
  160.8 0.8 copy.36
  161.6 0.0 copy-done
  161.6 0.8 copy.37
  162.4 0.0 copy-done.3
  162.4 0.6 copy.38
Async XLA Ops:
  153.4 6.6 %copy-start.2 = (bf16[256,1024]{1,0:T(8,128)(2,1)S(1)}, bf16[256,1024]{1,0:T(8,128)(2,1)}, u32[]{:S(2)}) copy-start(bf16[256,1024]{1,0:T(8,128)(2,1)} %get-tuple-element.68) | copy-start | bytes 1572868
  153.4 7.4 %copy-start.1 = (bf16[256,1024]{1,0:T(8,128)(2,1)S(1)}, bf16[256,1024]{1,0:T(8,128)(2,1)}, u32[]{:S(2)}) copy-start(bf16[256,1024]{1,0:T(8,128)(2,1)} %get-tuple-element.69) | copy-start | bytes 1572868
  156.0 5.6 %copy-start = (f32[32,4096]{1,0:T(8,128)S(1)}, f32[32,4096]{1,0:T(8,128)}, u32[]{:S(2)}) copy-start(f32[32,4096]{1,0:T(8,128)} %get-tuple-element.26) | copy-start | bytes 1572868
  158.0 4.4 %copy-start.3 = (f32[2,256]{1,0:T(2,128)S(1)}, f32[2,256]{1,0:T(2,128)}, u32[]{:S(2)}) copy-start(f32[2,256]{1,0:T(2,128)} %get-tuple-element.82) | copy-start | bytes 6148

commit v2 on v1

--- a/solution.py
+++ b/solution.py
@@ -328,43 +328,38 @@
 CHUNK = 32
 VMEM_BYTES = 62 * 1024 * 1024
 UNIT_ORDER = (
-    "wvxy",
     "xywv",
-    "yxwv",
+    "xwyv",
+    "ywxv",
     "wvxy",
     "yxwv",
     "wvyx",
-    "xywv",
-    "yxwv",
+    "xwvy",
     "yxwv",
     "xywv",
+    "ywxv",
+    "yxwv",
     "xywv",
-    "yxwv",
 )
 SLOTS = (
-    (0, 1, 10, 11, 20, 21,),
+    (0, 1, 20, 21, 30, 31,),
     (),
     (),
+    (10, 40, 50,),
+    (2, 22, 32,),
     (),
+    (3, 11, 23,),
+    (33, 41, 60,),
+    (12, 42,),
+    (34,),
+    (4, 70, 13, 52,),
+    (71,),
+    (43, 62, 24,),
     (),
-    (),
-    (30, 31, 40, 41, 60, 61,),
-    (2, 3, 12, 13, 22, 23,),
-    (),
-    (),
-    (),
-    (),
-    (70,),
-    (50, 90, 62, 91, 63, 42, 43, 51, 32, 33, 24, 4, 14,),
-    (),
-    (),
-    (71, 72, 80, 64,),
-    (5, 25, 15, 92,),
-    (6, 100, 93, 44,),
-    (73, 52, 81, 82,),
-    (26, 74, 16, 65,),
-    (53, 34, 110, 94, 102, 83, 66, 101, 45, 84, 35, 75, 103, 111, 36,),
-    (112, 46, 95, 104, 76, 85, 54, 113, 114, 96, 55, 86, 105, 56, 115, 106, 116,),
+    (90,),
+    (44, 72,),
+    (61, 91, 35, 25, 120, 14, 73, 5, 26, 74, 92, 6, 80, 63, 81, 100, 64, 93, 36, 121, 45, 15, 110, 82, 65, 51, 75, 102, 46, 122, 83, 16,),
+    (76, 101, 84, 111, 66, 94, 112, 53, 54, 103, 104, 123, 85, 113, 114, 124, 55, 95, 86, 105, 56, 96, 115, 106, 116,),
 )
 
 
@@ -393,8 +388,9 @@
 def layer_kernel(
     doc, tok, cot, gain_a, gain_b, gain_c, gain_d, bias_up, bias_down,
     wq_hbm, wk_hbm, wv_hbm, wo_hbm, wu_hbm, wd_hbm,
-    out, grad_tok, rms, o_down, o_up, o_late, o_aux,
-    wq, wk, wv, wo, wu, wd, xin, q_t, k_t, v_t, k_n, v_n, mask, attn_t, attn_nat, attn_oth,
+    out, grad_tok, rms, o_down, o_up, o_out, o_query, o_key, o_value,
+    small_up, small_down, small_a, small_b, small_c, small_d,
+    fin_up, wq, wk, wv, wo, wu, wd, xin, q_t, k_t, v_t, k_n, v_n, mask, attn_t, attn_nat, attn_oth,
     branch, hid, xm, act, g_t, part_send, part_recv, part_own, nat, gb_t, gba_t, ga_t,
     rope, lse, stat, s_down, r1_down, r2_down, r3_down, r4_down, r1_up, r2_up, r3_up, r4_up,
     r1_late, r2_late, r3_late, r4_late, fin_down, fin_late, rec_down, rec_late, aux_s, aux_r,
@@ -716,11 +712,13 @@
             add_rows(n, kept(n, k) + bit * count, k, bit * count, count)
         else:
             cols = pl.ds(c0, width)
-            dst = fin_down if n < 4 else o_up if n < 8 else fin_late
+            dst = fin_down if n < 4 else fin_up if n < 8 else fin_late
             dst[:, cols] = refs[0][pl.ds(al(kept(n, 4), rows), rows), cols].astype(F32) + refs[4][
                 :, cols
             ].astype(F32)
-            if dst is not o_up:
+            if dst is fin_up:
+                o_up[c0 : c0 + width, :] = fin_up[:, cols].T
+            else:
                 final_copy(n).start()
 
     oth_cut = pl.ds(al(other * 32, 32), 32)
@@ -732,10 +730,26 @@
         src, dst = (fin_down, rec_down) if n < 4 else (fin_late, rec_late)
         return to_core(14 + n, src.at[oth_cut, cols], dst.at[:, cols])
 
+    aux_peers = (core_peer, x_peer, y_peer, z_low, z_high)
+
+    def aux_copy(k):
+        return pltpu.make_async_remote_copy(
+            src_ref=aux_s.at[k], dst_ref=aux_r.at[k], send_sem=a_send.at[k],
+            recv_sem=a_recv.at[k], device_id=aux_peers[k], device_id_type=MESH_ID,
+        )
+
+    def aux_end(k):
+        aux_copy(k).wait_recv()
+        aux_s[k + 1] = aux_s[k] + aux_r[k]
+        if k < 4:
+            aux_copy(k + 1).start()
+
     def slot(i):
         for code in SLOTS[i]:
             n, k = code // 10, code % 10
-            if k < 2:
+            if n == 12:
+                aux_end(k)
+            elif k < 2:
                 unit_copy(n, k).start()
             else:
                 serve(n, k - 2)
@@ -783,7 +797,7 @@
     lax.fori_loop(0, 4, lambda i, c: (mlp_back(own_tok, part_own, i), c)[1], 0)
     ones = jnp.ones((16, PACK), BF16)
     for i in range(2):
-        aux_s[0, pl.ds(5 + 2 * b + i, 1), :] = mm_nt(ones, g_t[i * 1024 : i * 1024 + 1024, :])[0:1]
+        aux_s[0, pl.ds(8 + 2 * b + i, 1), :] = mm_nt(ones, g_t[i * 1024 : i * 1024 + 1024, :])[0:1]
     slot(6)
     mlp_back_copy.wait()
 
@@ -898,23 +912,8 @@
 
     aux_s[0, 1:2, :] = lax.fori_loop(0, TOK // CHUNK, token_back, zero_row)
 
-    aux_peers = (core_peer, x_peer, y_peer, z_low, z_high)
-
-    def aux_copy(k):
-        return pltpu.make_async_remote_copy(
-            src_ref=aux_s.at[k], dst_ref=aux_r.at[k], send_sem=a_send.at[k],
-            recv_sem=a_recv.at[k], device_id=aux_peers[k], device_id_type=MESH_ID,
-        )
-
     aux_copy(0).start()
-    for k in range(5):
-        slot(16 + k)
-        aux_copy(k).wait_recv()
-        aux_s[k + 1] = aux_s[k] + aux_r[k]
-        if k < 4:
-            aux_copy(k + 1).start()
-    o_aux[...] = aux_s[5]
-    slot(21)
+    slot(16)
     for n in range(4):
         final_copy(n).wait()
 
@@ -925,7 +924,15 @@
         return carry
 
     lax.fori_loop(0, 16, place_down, 0)
-    slot(22)
+    slot(17)
+    device = dp * 2 + b
+    at = pl.ds(al(device // 4 * 128, 128), 128)
+    lines = pltpu.roll(aux_s[5, 0:8, at], lax.rem(128 - lax.rem(device, 4) * 32, 128), 1)
+    for i, ref in enumerate((small_down, small_a, small_b, small_c, small_d)):
+        ref[...] = lines[i, :32]
+    lines = aux_s[5, 8:16, pl.ds(al(lax.rem(dp, 8) * 128, 128), 128)]
+    chosen = lax.broadcasted_iota(jnp.int32, (8, 128), 0) == 2 * b + dp // 8
+    small_up[...] = jnp.sum(jnp.where(chosen, lines, 0.0), axis=0)
     for n in range(12):
         for k in range(5):
             unit_copy(n, k).wait_send()
@@ -934,8 +941,28 @@
     for i in range(4):
         final_copy(8 + i).wait()
         cols = slice(i * 512, i * 512 + 512)
-        o_late[i, :, pl.ds(own_cols, HALF_D)] = fin_late[own_cut, cols]
-        o_late[i, :, pl.ds(oth_cols, HALF_D)] = rec_late[:, cols]
+        dst = (o_out, o_query, o_key, o_value)[i]
+        dst[:, pl.ds(own_cols, HALF_D)] = fin_late[own_cut, cols]
+        dst[:, pl.ds(oth_cols, HALF_D)] = rec_late[:, cols]
+
+
+def finish_kernel(*refs):
+    count = len(refs) // 3
+    sems = refs[-1]
+    gets = [
+        pltpu.make_async_copy(refs[i], refs[2 * count + i], sems.at[0, i]) for i in range(count)
+    ]
+    puts = [
+        pltpu.make_async_copy(refs[2 * count + i], refs[count + i], sems.at[1, i])
+        for i in range(count)
+    ]
+    for copy in gets:
+        copy.start()
+    for get, put in zip(gets, puts):
+        get.wait()
+        put.start()
+    for copy in puts:
+        copy.wait()
 
 
 def layer_on_device(
@@ -951,6 +978,7 @@
     dma = pltpu.SemaphoreType.DMA
     vmem = pl.BlockSpec(memory_space=pltpu.VMEM)
     scratch = [
+        v32(128, 1024),
         v16(1024, 512), v16(1024, 512), v16(1024, 512), v16(1024, 1024),
         v16(1024, 2048), v16(2048, 1024),
         v16(512, 1024),
@@ -968,21 +996,16 @@
         v32(6, 16, 1024), v32(5, 16, 1024),
         dma((36,)), dma((26,)), dma((26,)), dma((12, 5)), dma((12, 5)), dma((5,)), dma((5,)),
     ]
-    out, grad_tok, rms, down, up, late, aux = pl.pallas_call(
+    shapes = [((TOK, D), BF16)] * 2 + [((2, TOK), F32), ((32, FF), F32), ((D, 128), F32)]
+    shapes += [((32, D), F32)] * 4 + [((128,), F32)] + [((32,), F32)] * 5
+    shapes = [jax.ShapeDtypeStruct(*shape) for shape in shapes]
+    results = pl.pallas_call(
         layer_kernel,
-        out_shape=(
-            jax.ShapeDtypeStruct((TOK, D), BF16),
-            jax.ShapeDtypeStruct((TOK, D), BF16),
-            jax.ShapeDtypeStruct((2, TOK), F32),
-            jax.ShapeDtypeStruct((32, FF), F32),
-            jax.ShapeDtypeStruct((128, D), F32),
-            jax.ShapeDtypeStruct((4, 32, D), F32),
-            jax.ShapeDtypeStruct((16, D), F32),
-        ),
+        out_shape=shapes,
         in_specs=[pl.BlockSpec(memory_space=pltpu.SMEM)]
         + [vmem] * 8
         + [pl.BlockSpec(memory_space=pl.ANY)] * 6,
-        out_specs=[vmem] * 7,
+        out_specs=[vmem] * 15,
         scratch_shapes=scratch,
         compiler_params=pltpu.CompilerParams(
             collective_id=0, has_side_effects=True, vmem_limit_bytes=VMEM_BYTES
@@ -993,16 +1016,16 @@
         bias_up.reshape(32, 128), bias_down[None],
         w_query, w_key, w_value, w_out, w_up, w_down,
     )
-    dp = lax.axis_index("dp")
-    b = lax.axis_index("blk")
-    at = (dp * 2 + b) * 32
-    small = lax.dynamic_slice(aux, (0, at), (5, 32))
-    bias_rows = lax.dynamic_slice(
-        aux, (5 + 2 * b + dp // 8, lax.rem(dp, 8) * 128), (1, 128)
-    )[0]
+    hbm = pl.BlockSpec(memory_space=pltpu.HBM)
+    out, grad_tok, rms, gd, gu, go, gq, gk, gv, small_up, small_down, sa, sb, sc, sd = pl.pallas_call(
+        finish_kernel,
+        out_shape=shapes,
+        in_specs=[hbm] * 15,
+        out_specs=[hbm] * 15,
+        scratch_shapes=[pltpu.VMEM(s.shape, s.dtype) for s in shapes] + [dma((2, 15))],
+    )(*results)
     return (
-        out, grad_tok, late[1].T, late[2].T, late[3].T, late[0].T, up.T, down.T,
-        bias_rows, small[0], small[1], small[2], small[3], small[4], rms,
+        out, grad_tok, gq.T, gk.T, gv.T, go.T, gu, gd.T, small_up, small_down, sa, sb, sc, sd, rms
     )
 
 

time: 163 us -> 144 us (0.88)
  Pallas kernels: 153 us -> 143 us
  local copies, waits for them, and re-layouts: 9.58 us -> 0 us
    pallas_call x1 -> x2, Pallas kernels: 153 us -> 143 us  [the longest x1 141 us: layer_on_device(): pl.pallas_call(layer_kernel, out_shape=shapes, in_specs=[pl.BlockSpec(mem...]
    unnamed x13 -> x0, local copies, waits for them, and re-layouts: 5.01 us -> none
    transpose x1 -> x0, local copies, waits for them, and re-layouts: 1.95 us -> none  [layer_on_device(): late[0]]
    squeeze x2 -> x0, local copies, waits for them, and re-layouts: 1.88 us -> none  [the longest x1 1.35 us: layer_on_device(): lax.dynamic_slice(aux, (5 + 2 * b + dp // 8, lax.rem(dp, 8) * 128), (1, 1...]
where the time goes in v2:
time: 144 us
  Pallas kernels  143 us (99%)
    pallas_call x1, Pallas kernels, layer_on_device(): pl.pallas_call(layer_kernel, out_shape=shapes, in_specs=[pl.BlockSpec(mem...  141 us

profile of v2, /device:TPU:0, one launch (start us, length us, event | category | flops | bytes accessed | tf_op | source)
XLA Modules:
  0.0 144.1 jit_solution(15533714064476680650)
XLA Ops:
  0.7 140.5 %shard_map.262 = (bf16[256,1024]{1,0:T(8,128)(2,1)}, bf16[256,1024]{1,0:T(8,128)(2,1)}, f32[2,256]{1,0:T(2,128)}, f32[32,4096]{1,0:T(8,128)}, f32[1024,128]{1,0:...) custom-call(s32[1,4]{1,0:T(1,128)} %doc.1, ...), custom_call_target="tpu_custom_call" | custom-call | tf_op jit(solution)/shard_map/pallas_call | solution.py:1002
  141.2 2.8 %shard_map.263 = (bf16[256,1024]{1,0:T(8,128)(2,1)}, bf16[256,1024]{1,0:T(8,128)(2,1)}, f32[2,256]{1,0:T(2,128)}, f32[32,4096]{1,0:T(8,128)}, f32[1024,128]{1,0:...) custom-call(bf16[256,1024]{1,0:T(8,128)(2,1)} %get-tuple-element.45., ...), custom_call_target="tpu_custom_call" | custom-call | tf_op jit(solution)/shard_map/pallas_call | solution.py:1020

commit v3 on v2

--- a/solution.py
+++ b/solution.py
@@ -325,7 +325,7 @@
 FF = 4096
 HALF_FF = 2048
 HALF_D = 512
-CHUNK = 32
+CHUNK = 128
 VMEM_BYTES = 62 * 1024 * 1024
 UNIT_ORDER = (
     "xywv",
@@ -522,17 +522,21 @@
 
     def attend(p, carry):
         slab_cols = pl.ds(al(p * 128, 128), 128)
-        for which in range(2):
-            rows = pl.ds(al(p * 128 + which * 64, 64), 64)
-            for block in range(2):
-                cols = slice(block * TOK, block * TOK + TOK)
-                keys = (block + 1) * TOK
-                scores = mm(k_n[:keys, slab_cols], slab(q_t[rows, cols], which)) + mask[:keys, cols]
-                top = jnp.max(scores, axis=0, keepdims=True)
-                weights = jnp.exp(scores - top)
-                total = jnp.sum(weights, axis=0, keepdims=True)
-                attn_t[rows, cols] = mm(v_t[rows, :keys], weights.astype(BF16)) * (1.0 / total)
-                lse[pl.ds(p * 2 + which, 1), cols] = top + jnp.log(total)
+        parts = [
+            (w, pl.ds(al(p * 128 + w * 64, 64), 64), slice(i * TOK, i * TOK + TOK), (i + 1) * TOK)
+            for i in (1, 0)
+            for w in (0, 1)
+        ]
+        scores = [
+            mm(k_n[:keys, slab_cols], slab(q_t[rows, cols], w)) + mask[:keys, cols]
+            for w, rows, cols, keys in parts
+        ]
+        tops = [jnp.max(score, axis=0, keepdims=True) for score in scores]
+        weights = [jnp.exp(score - top) for score, top in zip(scores, tops)]
+        totals = [jnp.sum(weight, axis=0, keepdims=True) for weight in weights]
+        for (w, rows, cols, keys), weight, top, total in zip(parts, weights, tops, totals):
+            attn_t[rows, cols] = mm(v_t[rows, :keys], weight.astype(BF16)) * (1.0 / total)
+            lse[pl.ds(p * 2 + w, 1), cols] = top + jnp.log(total)
         attn_nat[:, slab_cols] = attn_t[pl.ds(al(p * 128, 128), 128), :].T.astype(BF16)
         to_core(
             1 + p, attn_nat.at[pl.ds(oth_tok, TOK), slab_cols], attn_oth.at[:, slab_cols]
@@ -569,10 +573,10 @@
     xm_copy.start()
 
     def up_step(tok_at, i):
-        cols = pl.ds(al(i * 256, 256), 256)
+        cols = pl.ds(al(i * 1024, 1024), 1024)
         rows = pl.ds(tok_at, TOK)
         bias = jnp.concatenate(
-            [bias_up[pl.ds(4 * i + b, 1), :], bias_up[pl.ds(4 * i + 2 + b, 1), :]], axis=1
+            [bias_up[pl.ds(16 * i + 2 * j + b, 1), :] for j in range(8)], axis=1
         )
         pre = mm(xm[rows, :], wu[:, cols]) + bias
         square = pre * pre
@@ -585,19 +589,19 @@
         g_t[cols, rows] = slope.astype(BF16).T
 
     lax.fori_loop(0, 16, lambda j, c: (up_copy(j).wait(), c)[1], 0)
-    lax.fori_loop(0, 8, lambda i, c: (up_step(own_tok, i), c)[1], 0)
+    lax.fori_loop(0, 2, lambda i, c: (up_step(own_tok, i), c)[1], 0)
     xm_copy.wait()
-    lax.fori_loop(0, 8, lambda i, c: (up_step(oth_tok, i), c)[1], 0)
+    lax.fori_loop(0, 2, lambda i, c: (up_step(oth_tok, i), c)[1], 0)
     lax.fori_loop(0, 16, lambda j, c: (down_copy(j).wait(), c)[1], 0)
 
     def down_step(tok_at, dst, i):
-        cols = pl.ds(al(i * 256, 256), 256)
+        cols = pl.ds(al(i * 1024, 1024), 1024)
         dst[:, cols] = mm(act[pl.ds(tok_at, TOK), :], wd[:, cols])
 
-    lax.fori_loop(0, 4, lambda i, c: (down_step(oth_tok, part_send, i), c)[1], 0)
+    down_step(oth_tok, part_send, 0)
     mlp_copy = to_core(6, part_send, part_recv)
     mlp_copy.start()
-    lax.fori_loop(0, 4, lambda i, c: (down_step(own_tok, part_own, i), c)[1], 0)
+    down_step(own_tok, part_own, 0)
     mlp_copy.wait()
 
     def post_mlp(i, carry):
@@ -775,11 +779,11 @@
         slot(first // 2)
 
     def act_back(i, carry):
-        rows = pl.ds(al(i * 256, 256), 256)
+        rows = pl.ds(al(i * 512, 512), 512)
         g_t[rows, :] = (mm(wd[rows, :], gb_t[...]) * g_t[rows, :].astype(F32)).astype(BF16)
         return carry
 
-    lax.fori_loop(0, 8, act_back, 0)
+    lax.fori_loop(0, 4, act_back, 0)
     slot(2)
     for first in (0, 2):
         for n in range(4, 8):
@@ -787,14 +791,14 @@
         slot(3 + first // 2)
 
     def mlp_back(tok_at, dst, i):
-        at = pl.ds(al(i * 256, 256), 256)
+        at = pl.ds(al(i * 512, 512), 512)
         dst[:, at] = mm(wu[at, :], g_t[:, pl.ds(tok_at, TOK)]).T
 
-    lax.fori_loop(0, 4, lambda i, c: (mlp_back(oth_tok, part_send, i), c)[1], 0)
+    lax.fori_loop(0, 2, lambda i, c: (mlp_back(oth_tok, part_send, i), c)[1], 0)
     mlp_back_copy = to_core(8, part_send, part_recv)
     mlp_back_copy.start()
     slot(5)
-    lax.fori_loop(0, 4, lambda i, c: (mlp_back(own_tok, part_own, i), c)[1], 0)
+    lax.fori_loop(0, 2, lambda i, c: (mlp_back(own_tok, part_own, i), c)[1], 0)
     ones = jnp.ones((16, PACK), BF16)
     for i in range(2):
         aux_s[0, pl.ds(8 + 2 * b + i, 1), :] = mm_nt(ones, g_t[i * 1024 : i * 1024 + 1024, :])[0:1]
@@ -834,38 +838,56 @@
 
     def attend_back(p, carry):
         slab_cols = pl.ds(al(p * 128, 128), 128)
-        for which in range(2):
-            rows = pl.ds(al(p * 128 + which * 64, 64), 64)
-            to = pl.ds(al(own_cols + p * 128 + which * 64, 64), 64)
-            grads_k, grads_v, grads_q = [], [], []
-            for block in range(2):
-                cols = slice(block * TOK, block * TOK + TOK)
-                keys = (block + 1) * TOK
-                q_rows = q_t[rows, cols]
-                g_rows = ga_t[rows, cols]
-                delta = jnp.sum(g_rows.astype(F32) * attn_t[rows, cols], axis=0, keepdims=True)
-                scores = mm(k_n[:keys, slab_cols], slab(q_rows, which)) + mask[:keys, cols]
-                probs = jnp.exp(scores - lse[pl.ds(p * 2 + which, 1), cols])
-                g_probs = mm(v_n[:keys, slab_cols], slab(g_rows, which))
-                g_scores = (probs * (g_probs - delta)).astype(BF16)
-                grads_q.append(mm(k_t[rows, :keys], g_scores) * 0.125)
-                grads_k.append(mm_nt(q_rows, g_scores))
-                grads_v.append(mm_nt(g_rows, probs.astype(BF16)))
-            for parts, dst in ((grads_q, gq), (grads_k, gk)):
-                if dst is gq:
-                    full = jnp.concatenate(parts, axis=1)
-                else:
-                    full = jnp.concatenate(
-                        [parts[0] + parts[1][:, :TOK], parts[1][:, TOK:]], axis=1
-                    )
+        parts = [
+            (w, pl.ds(al(p * 128 + w * 64, 64), 64), slice(i * TOK, i * TOK + TOK), (i + 1) * TOK)
+            for w in (0, 1)
+            for i in (0, 1)
+        ]
+        deltas = [
+            jnp.sum(ga_t[rows, cols].astype(F32) * attn_t[rows, cols], axis=0, keepdims=True)
+            for w, rows, cols, keys in parts
+        ]
+        scores = [
+            mm(k_n[:keys, slab_cols], slab(q_t[rows, cols], w)) + mask[:keys, cols]
+            for w, rows, cols, keys in parts
+        ]
+        g_probs = [
+            mm(v_n[:keys, slab_cols], slab(ga_t[rows, cols], w)) for w, rows, cols, keys in parts
+        ]
+        probs = [
+            jnp.exp(score - lse[pl.ds(p * 2 + part[0], 1), part[2]])
+            for score, part in zip(scores, parts)
+        ]
+        g_scores = [
+            (prob * (g_prob - delta)).astype(BF16)
+            for prob, g_prob, delta in zip(probs, g_probs, deltas)
+        ]
+        grads_q = [
+            mm(k_t[rows, :keys], g_score) * 0.125
+            for (w, rows, cols, keys), g_score in zip(parts, g_scores)
+        ]
+        grads_k = [
+            mm_nt(q_t[rows, cols], g_score)
+            for (w, rows, cols, keys), g_score in zip(parts, g_scores)
+        ]
+        grads_v = [
+            mm_nt(ga_t[rows, cols], prob.astype(BF16))
+            for (w, rows, cols, keys), prob in zip(parts, probs)
+        ]
+
+        def both(first, second):
+            return jnp.concatenate([first + second[:, :TOK], second[:, TOK:]], axis=1)
+
+        cos, sin = rope[0], rope[1]
+        for w in range(2):
+            to = pl.ds(al(own_cols + p * 128 + w * 64, 64), 64)
+            full_q = jnp.concatenate(grads_q[2 * w : 2 * w + 2], axis=1)
+            for full, dst in ((full_q, gq), (both(*grads_k[2 * w : 2 * w + 2]), gk)):
                 low, high = full[:32], full[32:]
-                cos, sin = rope[0], rope[1]
                 dst[to, :] = jnp.concatenate(
                     [low * cos + high * sin, high * cos - low * sin], axis=0
                 ).astype(BF16)
-            gv[to, :] = jnp.concatenate(
-                [grads_v[0] + grads_v[1][:, :TOK], grads_v[1][:, TOK:]], axis=1
-            ).astype(BF16)
+            gv[to, :] = both(*grads_v[2 * w : 2 * w + 2]).astype(BF16)
         return carry
 
     lax.fori_loop(0, 2, attend_back, 0)
@@ -880,14 +902,14 @@
     slot(11)
 
     def in_back(tok_at, dst, i):
-        at = pl.ds(al(i * 256, 256), 256)
+        at = pl.ds(al(i * 512, 512), 512)
         cols = pl.ds(tok_at, TOK)
         total = mm(wq[at, :], gq[own_heads, cols])
         total += mm(wk[at, :], gk[own_heads, cols])
         total += mm(wv[at, :], gv[own_heads, cols])
         dst[:, at] = total.T
 
-    lax.fori_loop(0, 4, lambda i, c: (in_back(oth_tok, part_send, i), c)[1], 0)
+    lax.fori_loop(0, 2, lambda i, c: (in_back(oth_tok, part_send, i), c)[1], 0)
     in_back_copy = to_core(13, part_send, part_recv)
     in_back_copy.start()
     slot(12)
@@ -897,7 +919,7 @@
         for n, lhs in zip((9, 10, 11), (gq, gk, gv)):
             weight_grad(n, first, first + 2, lhs, xin, own_cols)
         slot(13 + first // 2)
-    lax.fori_loop(0, 4, lambda i, c: (in_back(own_tok, part_own, i), c)[1], 0)
+    lax.fori_loop(0, 2, lambda i, c: (in_back(own_tok, part_own, i), c)[1], 0)
     slot(15)
     in_back_copy.wait()
 

time: 144 us -> 136 us (0.944)
  Pallas kernels: 143 us -> 135 us
    pallas_call x1, Pallas kernels: 141 us -> 132 us  [layer_on_device(): pl.pallas_call(layer_kernel, out_shape=shapes, in_specs=[pl.BlockSpec(mem...]
where the time goes in v3:
time: 136 us
  Pallas kernels  135 us (99%)
    pallas_call x1, Pallas kernels, layer_on_device(): pl.pallas_call(layer_kernel, out_shape=shapes, in_specs=[pl.BlockSpec(mem...  132 us
    pallas_call x1, Pallas kernels, layer_on_device(): pl.pallas_call(finish_kernel, out_shape=shapes, in_specs=[hbm] * 15, out_...  2.82 us

profile of v3, /device:TPU:0, one launch (start us, length us, event | category | flops | bytes accessed | tf_op | source)
XLA Modules:
  0.0 135.6 jit_solution(11653387729429108301)
XLA Ops:
  0.7 132.0 %shard_map.262 = (bf16[256,1024]{1,0:T(8,128)(2,1)}, bf16[256,1024]{1,0:T(8,128)(2,1)}, f32[2,256]{1,0:T(2,128)}, f32[32,4096]{1,0:T(8,128)}, f32[1024,128]{1,0:...) custom-call(s32[1,4]{1,0:T(1,128)} %doc.1, ...), custom_call_target="tpu_custom_call" | custom-call | tf_op jit(solution)/shard_map/pallas_call | solution.py:1024
  132.6 2.8 %shard_map.263 = (bf16[256,1024]{1,0:T(8,128)(2,1)}, bf16[256,1024]{1,0:T(8,128)(2,1)}, f32[2,256]{1,0:T(2,128)}, f32[32,4096]{1,0:T(8,128)}, f32[1024,128]{1,0:...) custom-call(bf16[256,1024]{1,0:T(8,128)(2,1)} %get-tuple-element.45., ...), custom_call_target="tpu_custom_call" | custom-call | tf_op jit(solution)/shard_map/pallas_call | solution.py:1042

commit v4 on v3

--- a/solution.py
+++ b/solution.py
@@ -328,38 +328,43 @@
 CHUNK = 128
 VMEM_BYTES = 62 * 1024 * 1024
 UNIT_ORDER = (
+    "wxyv",
+    "ywxv",
+    "yxwv",
+    "wyxv",
+    "wyv",
+    "ywv",
+    "ywv",
+    "ywv",
+    "ywxv",
+    "yxwv",
+    "wxyv",
     "xywv",
     "xwyv",
-    "ywxv",
-    "wvxy",
-    "yxwv",
-    "wvyx",
-    "xwvy",
-    "yxwv",
     "xywv",
-    "ywxv",
     "yxwv",
     "xywv",
 )
 SLOTS = (
-    (0, 1, 20, 21, 30, 31,),
+    (0, 1, 10, 11,),
     (),
     (),
-    (10, 40, 50,),
-    (2, 22, 32,),
+    (20, 30,),
+    (2, 12,),
     (),
-    (3, 11, 23,),
-    (33, 41, 60,),
-    (12, 42,),
-    (34,),
-    (4, 70, 13, 52,),
-    (71,),
-    (43, 62, 24,),
+    (21,),
     (),
-    (90,),
-    (44, 72,),
-    (61, 91, 35, 25, 120, 14, 73, 5, 26, 74, 92, 6, 80, 63, 81, 100, 64, 93, 36, 121, 45, 15, 110, 82, 65, 51, 75, 102, 46, 122, 83, 16,),
-    (76, 101, 84, 111, 66, 94, 112, 53, 54, 103, 104, 123, 85, 113, 114, 124, 55, 95, 86, 105, 56, 96, 115, 106, 116,),
+    (3, 13,),
+    (22, 31, 80, 32,),
+    (),
+    (),
+    (100,),
+    (),
+    (14, 81, 23,),
+    (40, 82, 50, 33,),
+    (34, 102,),
+    (41, 51, 83, 160, 42, 4, 101, 84, 52, 43, 53, 24, 60, 103, 44, 15, 61, 5, 35, 54, 45, 70, 62, 104, 16, 110, 161, 111, 63, 85, 25, 6, 72, 120, 112, 105, 36, 71, 121, 113, 162, 64, 55, 90, 114, 130, 86, 122, 91, 73, 131, 26,),
+    (123, 74, 106, 140, 92, 132, 65, 163, 150, 93, 133, 115, 75, 141, 142, 94, 164, 151, 134, 116, 152, 124, 95, 143, 144, 135, 96, 153, 154, 136, 145, 125, 155, 146, 126, 156,),
 )
 
 
@@ -390,11 +395,11 @@
     wq_hbm, wk_hbm, wv_hbm, wo_hbm, wu_hbm, wd_hbm,
     out, grad_tok, rms, o_down, o_up, o_out, o_query, o_key, o_value,
     small_up, small_down, small_a, small_b, small_c, small_d,
-    fin_up, wq, wk, wv, wo, wu, wd, xin, q_t, k_t, v_t, k_n, v_n, mask, attn_t, attn_nat, attn_oth,
+    wq, wk, wv, wo, wu, wd, xin, q_t, k_t, v_t, k_n, v_n, mask, attn_t, attn_nat, attn_oth,
     branch, hid, xm, act, g_t, part_send, part_recv, part_own, nat, gb_t, gba_t, ga_t,
-    rope, lse, stat, s_down, r1_down, r2_down, r3_down, r4_down, r1_up, r2_up, r3_up, r4_up,
+    rope, lse, stat, s_down, r1_down, r2_down, r3_down, r4_down, r1_up, r2_up, r3_up, xm_m, pre_m,
     r1_late, r2_late, r3_late, r4_late, fin_down, fin_late, rec_down, rec_late, aux_s, aux_r,
-    w_sem, c_send, c_recv, rs_send, rs_recv, a_send, a_recv,
+    w_sem, m_send, m_recv, c_send, c_recv, rs_send, rs_recv, a_send, a_recv,
 ):
     dp = lax.axis_index("dp")
     b = lax.axis_index("blk")
@@ -439,9 +444,6 @@
             w_sem.at[20 + j],
         )
 
-    lax.fori_loop(0, 16, lambda j, c: (up_copy(j).start(), c)[1], 0)
-    lax.fori_loop(0, 16, lambda j, c: (down_copy(j).start(), c)[1], 0)
-
     def to_core(k, src, dst):
         return pltpu.make_async_remote_copy(
             src_ref=src, dst_ref=dst, send_sem=c_send.at[k], recv_sem=c_recv.at[k],
@@ -511,6 +513,8 @@
 
     for copy in w_copies[:3]:
         copy.wait()
+    lax.fori_loop(0, 16, lambda j, c: (up_copy(j).start(), c)[1], 0)
+    lax.fori_loop(0, 16, lambda j, c: (down_copy(j).start(), c)[1], 0)
     project(own_tok)
     xin_copy.wait()
     project(oth_tok)
@@ -571,6 +575,11 @@
     own_rows_m = xm.at[pl.ds(own_tok, TOK)]
     xm_copy = to_core(5, own_rows_m, own_rows_m)
     xm_copy.start()
+    xm_mate = pltpu.make_async_remote_copy(
+        src_ref=own_rows_m, dst_ref=xm_m.at[pl.ds(own_tok, TOK)], send_sem=m_send.at[8],
+        recv_sem=m_recv.at[8], device_id=x_peer, device_id_type=MESH_ID,
+    )
+    xm_mate.start()
 
     def up_step(tok_at, i):
         cols = pl.ds(al(i * 1024, 1024), 1024)
@@ -595,19 +604,24 @@
     lax.fori_loop(0, 16, lambda j, c: (down_copy(j).wait(), c)[1], 0)
 
     def down_step(tok_at, dst, i):
-        cols = pl.ds(al(i * 1024, 1024), 1024)
-        dst[:, cols] = mm(act[pl.ds(tok_at, TOK), :], wd[:, cols])
-
-    down_step(oth_tok, part_send, 0)
-    mlp_copy = to_core(6, part_send, part_recv)
-    mlp_copy.start()
-    down_step(own_tok, part_own, 0)
-    mlp_copy.wait()
-
+        cols = slice(i * 512, i * 512 + 512)
+        dst[:, cols] = mm(act[pl.ds(tok_at, TOK), :], wd[:, cols]).astype(dst.dtype)
+
+    mlp_copies = [
+        to_core(k, part_send.at[:, pl.ds(i * 512, 512)], part_recv.at[:, pl.ds(i * 512, 512)])
+        for i, k in ((0, 6), (1, 31))
+    ]
+    for i in range(2):
+        down_step(oth_tok, part_send, i)
+        mlp_copies[i].start()
+    for i in range(2):
+        down_step(own_tok, part_own, i)
+    for copy in mlp_copies:
+        copy.wait()
     def post_mlp(i, carry):
         sum_bias, sum_gain = carry
         rows = pl.ds(al(i * CHUNK, CHUNK), CHUNK)
-        v = part_own[rows, :] + part_recv[rows, :] + bias_down[...]
+        v = part_own[rows, :] + part_recv[rows, :].astype(F32) + bias_down[...]
         square = jnp.mean(v * v, axis=-1, keepdims=True) + eps
         stat[1, rows, :] = jnp.broadcast_to(jnp.sqrt(square), (CHUNK, 128))
         r = lax.rsqrt(square)
@@ -620,35 +634,38 @@
             sum_gain + gain_part,
         )
 
+    def turn_and_send(dst, i, k):
+        tok_cols = pl.ds(al(own_tok + i * CHUNK, CHUNK), CHUNK)
+        for j in range(4):
+            cols = slice(j * 256, j * 256 + 256)
+            dst[cols, tok_cols] = nat[i * CHUNK : i * CHUNK + CHUNK, cols].T
+        part = dst.at[:, tok_cols]
+        copy = to_core(k, part, part)
+        copy.start()
+        return copy
+
     zero_row = jnp.zeros((1, D), F32)
-    sum_bias_down, sum_gain_d = lax.fori_loop(0, TOK // CHUNK, post_mlp, (zero_row, zero_row))
+    sums = (zero_row, zero_row)
+    gb_copies = []
+    for i, k in ((0, 7), (1, 32)):
+        sums = post_mlp(i, sums)
+        gb_copies.append(turn_and_send(gb_t, i, k))
+    sum_bias_down, sum_gain_d = sums
     aux_s[0] = jnp.zeros((16, D), F32)
     aux_s[0, 0:1, :] = sum_bias_down
     aux_s[0, 4:5, :] = sum_gain_d
     for i in range(2):
         rms[i : i + 1, :] = stat[i].T[0:1, :]
 
-    def turn_to(dst):
-        def step(i, carry):
-            cols = pl.ds(al(i * 256, 256), 256)
-            dst[cols, pl.ds(own_tok, TOK)] = nat[:, cols].T
-            return carry
-
-        lax.fori_loop(0, 4, step, 0)
-
-    turn_to(gb_t)
-    own_gb = gb_t.at[:, pl.ds(own_tok, TOK)]
-    gb_copy = to_core(7, own_gb, own_gb)
-    gb_copy.start()
-    gb_copy.wait()
-
+    for copy in gb_copies:
+        copy.wait()
     down_refs = (s_down, r1_down, r2_down, r3_down, r4_down)
-    up_refs = (wd, r1_up, r2_up, r3_up, r4_up)
+    up_refs = (wd, r1_up, r2_up, r3_up)
     late_refs = (wu, r1_late, r2_late, r3_late, r4_late)
     units = (
         [(down_refs, 512 * i, 512, 64) for i in range(4)]
         + [(up_refs, 256 * i, 256, 128) for i in range(4)]
-        + [(late_refs, 512 * i, 512, 64) for i in range(4)]
+        + [(late_refs, 256 * i, 256, 64) for i in range(8)]
     )
     place = {
         "x": (x, 1, x_peer),
@@ -661,24 +678,24 @@
         return [place[letter] for letter in UNIT_ORDER[n]]
 
     def kept(n, steps):
-        rows = units[n][3]
-        return sum(
-            (axis[0] * (8 >> i) * rows for i, axis in enumerate(unit_axes(n)[:steps])), 0
-        )
+        axes = unit_axes(n)
+        step = 2 ** len(axes) // 2 * units[n][3]
+        return sum((axis[0] * (step >> i) for i, axis in enumerate(axes[:steps])), 0)
 
     def unit_copy(n, k):
         refs, c0, width, rows = units[n]
         axes = unit_axes(n)
+        span = 2 ** len(axes)
         cols = pl.ds(c0, width)
         if k < 2:
             bit, _, peer = axes[0]
             second = lax.rem(axes[1][0] + 1 + k, 2)
-            count = 4 * rows
+            count = span // 4 * rows
             src = refs[0].at[pl.ds(al(((1 - bit) * 2 + second) * count, count), count), cols]
             dst = refs[1].at[pl.ds(al(second * count, count), count), cols]
         else:
             bit, _, peer = axes[k - 1]
-            count = (16 >> k) * rows
+            count = (span >> k) * rows
             at = kept(n, k - 1) + (1 - bit) * count
             src = refs[0].at[pl.ds(al(at, count), count), cols]
             dst = refs[k].at[:, cols]
@@ -702,27 +719,29 @@
     def serve(n, k):
         refs, c0, width, rows = units[n]
         axes = unit_axes(n)
+        last = len(axes)
+        span = 2**last
         unit_copy(n, k).wait_recv()
         if k < 2:
             second = lax.rem(axes[1][0] + 1 + k, 2)
-            add_rows(n, kept(n, 1) + second * 4 * rows, 1, second * 4 * rows, 4 * rows)
+            count = span // 4 * rows
+            add_rows(n, kept(n, 1) + second * count, 1, second * count, count)
             if k == 0:
                 unit_copy(n, 2).start()
-        elif k < 4:
-            count = (8 >> k) * rows
+        elif k < last:
+            count = (span // 2 >> k) * rows
             bit = axes[k][0]
             add_rows(n, kept(n, k) + (1 - bit) * count, k, (1 - bit) * count, count)
             unit_copy(n, k + 1).start()
             add_rows(n, kept(n, k) + bit * count, k, bit * count, count)
         else:
             cols = pl.ds(c0, width)
-            dst = fin_down if n < 4 else fin_up if n < 8 else fin_late
-            dst[:, cols] = refs[0][pl.ds(al(kept(n, 4), rows), rows), cols].astype(F32) + refs[4][
-                :, cols
-            ].astype(F32)
-            if dst is fin_up:
-                o_up[c0 : c0 + width, :] = fin_up[:, cols].T
+            mine = refs[0][pl.ds(al(kept(n, last), rows), rows), cols].astype(F32)
+            total = mine + refs[last][:, cols].astype(F32)
+            if 4 <= n < 8:
+                o_up[c0 : c0 + width, :] = total.T
             else:
+                (fin_down if n < 4 else fin_late)[:, cols] = total
                 final_copy(n).start()
 
     oth_cut = pl.ds(al(other * 32, 32), 32)
@@ -751,58 +770,78 @@
     def slot(i):
         for code in SLOTS[i]:
             n, k = code // 10, code % 10
-            if n == 12:
+            if n == len(units):
                 aux_end(k)
             elif k < 2:
                 unit_copy(n, k).start()
             else:
                 serve(n, k - 2)
 
-    def weight_grad(n, first, last, lhs, rhs, rhs_at):
+    def weight_grad(n, first, last, *terms):
         refs, c0, width, rows = units[n]
         axes = unit_axes(n)
+        fixed = x if len(axes) == 3 else 0
+        tails = [0]
+        for axis in axes[2:]:
+            tails = [tail + p * axis[1] for tail in tails for p in range(2)]
+        count = len(tails) * rows
         for g in range(first, last):
             i = lax.rem(axes[0][0] + 1 + g // 2, 2)
             j = lax.rem(axes[1][0] + 1 + g % 2, 2)
-            base = i * axes[0][1] + j * axes[1][1]
-            tails = [p * axes[2][1] + q * axes[3][1] for p in range(2) for q in range(2)]
-            left = jnp.concatenate(
-                [lhs[pl.ds(al((base + tail) * rows, rows), rows), :] for tail in tails], axis=0
-            )
-            right = rhs[:, pl.ds(al(rhs_at, 256), width)]
-            at = pl.ds(al((i * 2 + j) * 4 * rows, 4 * rows), 4 * rows)
-            refs[0][at, pl.ds(c0, width)] = mm(left, right).astype(BF16)
+            base = i * axes[0][1] + j * axes[1][1] + fixed
+            total = None
+            for left, right in terms:
+                stack = jnp.concatenate([left(base + tail) for tail in tails], axis=0)
+                part = mm(stack, right)
+                total = part if total is None else total + part
+            at = pl.ds(al((i * 2 + j) * count, count), count)
+            refs[0][at, pl.ds(c0, width)] = total.astype(BF16)
+
+    def rows_of(ref, rows):
+        return lambda chip: ref[pl.ds(al(chip * rows, rows), rows), :]
 
     for first in (0, 2):
         for n in range(4):
-            weight_grad(n, first, first + 2, gb_t, act, 512 * n)
+            weight_grad(
+                n, first, first + 2, (rows_of(gb_t, 64), act[:, 512 * n : 512 * n + 512])
+            )
         slot(first // 2)
+
+    def mate_copy(k):
+        return pltpu.make_async_remote_copy(
+            src_ref=g_t.at[pl.ds(al((2 * k + 1 - x) * 128, 128), 128)],
+            dst_ref=pre_m.at[pl.ds(al(k * 128, 128), 128)],
+            send_sem=m_send.at[k], recv_sem=m_recv.at[k],
+            device_id=x_peer, device_id_type=MESH_ID,
+        )
 
     def act_back(i, carry):
         rows = pl.ds(al(i * 512, 512), 512)
         g_t[rows, :] = (mm(wd[rows, :], gb_t[...]) * g_t[rows, :].astype(F32)).astype(BF16)
+        for j in range(2):
+            mate_copy(2 * i + j).start()
         return carry
 
     lax.fori_loop(0, 4, act_back, 0)
+    xm_mate.wait()
+    mate_rows = xm_m.at[pl.ds(own_tok, TOK)]
+    xm_pass = to_core(30, mate_rows, mate_rows)
+    xm_pass.start()
     slot(2)
-    for first in (0, 2):
-        for n in range(4, 8):
-            weight_grad(n, first, first + 2, g_t, xm, 256 * (n - 4))
-        slot(3 + first // 2)
 
     def mlp_back(tok_at, dst, i):
         at = pl.ds(al(i * 512, 512), 512)
-        dst[:, at] = mm(wu[at, :], g_t[:, pl.ds(tok_at, TOK)]).T
+        dst[:, at] = mm(wu[at, :], g_t[:, pl.ds(tok_at, TOK)]).T.astype(dst.dtype)
 
     lax.fori_loop(0, 2, lambda i, c: (mlp_back(oth_tok, part_send, i), c)[1], 0)
     mlp_back_copy = to_core(8, part_send, part_recv)
     mlp_back_copy.start()
-    slot(5)
+    slot(3)
     lax.fori_loop(0, 2, lambda i, c: (mlp_back(own_tok, part_own, i), c)[1], 0)
     ones = jnp.ones((16, PACK), BF16)
     for i in range(2):
         aux_s[0, pl.ds(8 + 2 * b + i, 1), :] = mm_nt(ones, g_t[i * 1024 : i * 1024 + 1024, :])[0:1]
-    slot(6)
+    slot(4)
     mlp_back_copy.wait()
 
     def hidden_back(i, carry):
@@ -810,7 +849,7 @@
         rows = pl.ds(al(i * CHUNK, CHUNK), CHUNK)
         h = hid[rows, :]
         back, part_c = norm_back(
-            h, inv_rms(h), gain_c[...], part_own[rows, :] + part_recv[rows, :]
+            h, inv_rms(h), gain_c[...], part_own[rows, :] + part_recv[rows, :].astype(F32)
         )
         g_hidden = cot[rows, :].astype(F32) + back
         hid[rows, :] = g_hidden
@@ -819,22 +858,36 @@
         nat[rows, :] = back.astype(BF16)
         return sum_c + part_c, sum_b + part_b
 
-    sum_gain_c, sum_gain_b = lax.fori_loop(0, TOK // CHUNK, hidden_back, (zero_row, zero_row))
+    sums = (zero_row, zero_row)
+    gba_copies = []
+    for i, k in ((0, 9), (1, 33)):
+        sums = hidden_back(i, sums)
+        gba_copies.append(turn_and_send(gba_t, i, k))
+    sum_gain_c, sum_gain_b = sums
     aux_s[0, 3:4, :] = sum_gain_c
     aux_s[0, 2:3, :] = sum_gain_b
-    turn_to(gba_t)
-    own_gba = gba_t.at[:, pl.ds(own_tok, TOK)]
-    gba_copy = to_core(9, own_gba, own_gba)
-    gba_copy.start()
+    slot(5)
+    for copy in gba_copies:
+        copy.wait()
+
+    for n in (8, 9):
+        weight_grad(
+            n, 0, 4, (rows_of(gba_t, 64), attn_nat[:, 256 * (n - 8) : 256 * (n - 8) + 256])
+        )
+    slot(6)
+    ga_t[...] = mm(wo[pl.ds(own_cols, HALF_D), :], gba_t[...]).astype(BF16)
     slot(7)
-    gba_copy.wait()
-
-    weight_grad(8, 0, 4, gba_t, attn_nat, 0)
-    slot(8)
-    ga_t[...] = mm(wo[pl.ds(own_cols, HALF_D), :], gba_t[...]).astype(BF16)
-    slot(9)
-
-    gq, gk, gv = g_t.at[pl.ds(0, D)], g_t.at[pl.ds(D, D)], gb_t
+
+    def head_grad(off):
+        def rows(chip):
+            at = al(off + chip // 8 * HALF_D, HALF_D)
+            return act[pl.ds(al(lax.rem(chip, 8) * 64, 64), 64), pl.ds(at, HALF_D)]
+
+        return rows
+
+    own_q = pl.ds(al(own_cols, HALF_D), HALF_D)
+    own_k = pl.ds(al(D + own_cols, HALF_D), HALF_D)
+    gv = gb_t
 
     def attend_back(p, carry):
         slab_cols = pl.ds(al(p * 128, 128), 128)
@@ -881,61 +934,81 @@
         cos, sin = rope[0], rope[1]
         for w in range(2):
             to = pl.ds(al(own_cols + p * 128 + w * 64, 64), 64)
+            at = parts[2 * w][1]
             full_q = jnp.concatenate(grads_q[2 * w : 2 * w + 2], axis=1)
-            for full, dst in ((full_q, gq), (both(*grads_k[2 * w : 2 * w + 2]), gk)):
+            for full, dst in ((full_q, own_q), (both(*grads_k[2 * w : 2 * w + 2]), own_k)):
                 low, high = full[:32], full[32:]
-                dst[to, :] = jnp.concatenate(
+                act[at, dst] = jnp.concatenate(
                     [low * cos + high * sin, high * cos - low * sin], axis=0
                 ).astype(BF16)
             gv[to, :] = both(*grads_v[2 * w : 2 * w + 2]).astype(BF16)
         return carry
 
     lax.fori_loop(0, 2, attend_back, 0)
-    slot(10)
+    slot(8)
     lax.fori_loop(2, 4, attend_back, 0)
     own_heads = pl.ds(own_cols, HALF_D)
     head_copies = [
-        to_core(10 + i, ref.at[own_heads], ref.at[own_heads]) for i, ref in enumerate((gq, gk, gv))
+        to_core(10 + i, ref, ref)
+        for i, ref in enumerate((act.at[:, own_q], act.at[:, own_k], gv.at[own_heads]))
     ]
     for copy in head_copies:
         copy.start()
-    slot(11)
+    slot(9)
 
     def in_back(tok_at, dst, i):
         at = pl.ds(al(i * 512, 512), 512)
         cols = pl.ds(tok_at, TOK)
-        total = mm(wq[at, :], gq[own_heads, cols])
-        total += mm(wk[at, :], gk[own_heads, cols])
+        total = mm(wq[at, :], act[:, pl.ds(al(own_cols + tok_at, TOK), TOK)])
+        total += mm(wk[at, :], act[:, pl.ds(al(D + own_cols + tok_at, TOK), TOK)])
         total += mm(wv[at, :], gv[own_heads, cols])
-        dst[:, at] = total.T
+        dst[:, at] = total.T.astype(dst.dtype)
 
     lax.fori_loop(0, 2, lambda i, c: (in_back(oth_tok, part_send, i), c)[1], 0)
     in_back_copy = to_core(13, part_send, part_recv)
     in_back_copy.start()
-    slot(12)
+    slot(10)
     for copy in head_copies:
         copy.wait()
     for first in (0, 2):
-        for n, lhs in zip((9, 10, 11), (gq, gk, gv)):
-            weight_grad(n, first, first + 2, lhs, xin, own_cols)
-        slot(13 + first // 2)
+        for i, rows in enumerate((head_grad(0), head_grad(D), rows_of(gv, 64))):
+            for j in range(2):
+                cols = pl.ds(al(own_cols + 256 * j, 256), 256)
+                weight_grad(10 + 2 * i + j, first, first + 2, (rows, xin[:, cols]))
+        slot(11 + first // 2)
     lax.fori_loop(0, 2, lambda i, c: (in_back(own_tok, part_own, i), c)[1], 0)
-    slot(15)
+    slot(13)
     in_back_copy.wait()
 
     def token_back(i, carry):
         rows = pl.ds(al(i * CHUNK, CHUNK), CHUNK)
         v = tok[rows, :].astype(F32)
         back, part_a = norm_back(
-            v, inv_rms(v), gain_a[...], part_own[rows, :] + part_recv[rows, :]
+            v, inv_rms(v), gain_a[...], part_own[rows, :] + part_recv[rows, :].astype(F32)
         )
         grad_tok[rows, :] = (hid[rows, :] + back).astype(BF16)
         return carry + part_a
 
     aux_s[0, 1:2, :] = lax.fori_loop(0, TOK // CHUNK, token_back, zero_row)
+    slot(14)
+
+    for k in range(8):
+        mate_copy(k).wait()
+    xm_pass.wait()
+
+    def mate_pre(chip):
+        return pre_m[pl.ds(al(chip // 2 * 128, 128), 128), :]
+
+    for first in (0, 2):
+        for n in range(4, 8):
+            cols = slice(256 * (n - 4), 256 * (n - 4) + 256)
+            weight_grad(
+                n, first, first + 2, (rows_of(g_t, 128), xm[:, cols]), (mate_pre, xm_m[:, cols])
+            )
+        slot(15 + first // 2)
 
     aux_copy(0).start()
-    slot(16)
+    slot(17)
     for n in range(4):
         final_copy(n).wait()
 
@@ -946,7 +1019,7 @@
         return carry
 
     lax.fori_loop(0, 16, place_down, 0)
-    slot(17)
+    slot(18)
     device = dp * 2 + b
     at = pl.ds(al(device // 4 * 128, 128), 128)
     lines = pltpu.roll(aux_s[5, 0:8, at], lax.rem(128 - lax.rem(device, 4) * 32, 128), 1)
@@ -955,13 +1028,14 @@
     lines = aux_s[5, 8:16, pl.ds(al(lax.rem(dp, 8) * 128, 128), 128)]
     chosen = lax.broadcasted_iota(jnp.int32, (8, 128), 0) == 2 * b + dp // 8
     small_up[...] = jnp.sum(jnp.where(chosen, lines, 0.0), axis=0)
-    for n in range(12):
-        for k in range(5):
+    for n in range(len(units)):
+        for k in range(len(UNIT_ORDER[n]) + 1):
             unit_copy(n, k).wait_send()
     for k in range(5):
         aux_copy(k).wait_send()
     for i in range(4):
-        final_copy(8 + i).wait()
+        final_copy(8 + 2 * i).wait()
+        final_copy(9 + 2 * i).wait()
         cols = slice(i * 512, i * 512 + 512)
         dst = (o_out, o_query, o_key, o_value)[i]
         dst[:, pl.ds(own_cols, HALF_D)] = fin_late[own_cut, cols]
@@ -1000,7 +1074,6 @@
     dma = pltpu.SemaphoreType.DMA
     vmem = pl.BlockSpec(memory_space=pltpu.VMEM)
     scratch = [
-        v32(128, 1024),
         v16(1024, 512), v16(1024, 512), v16(1024, 512), v16(1024, 1024),
         v16(1024, 2048), v16(2048, 1024),
         v16(512, 1024),
@@ -1008,15 +1081,15 @@
         v32(512, 512), v32(512, 512), v16(512, 512), v16(256, 512),
         v32(256, 1024), v32(256, 1024), v16(512, 1024),
         v16(512, 2048), v16(2048, 512),
-        v32(256, 1024), v32(256, 1024), v32(256, 1024), v16(256, 1024),
+        v16(256, 1024), v16(256, 1024), v32(256, 1024), v16(256, 1024),
         v16(1024, 512), v16(1024, 512), v16(512, 512),
         v32(2, 32, 512), v32(8, 512), v32(2, 256, 128),
         v16(1024, 2048), v16(512, 2048), v16(256, 2048), v16(128, 2048), v16(64, 2048),
-        v16(1024, 1024), v16(512, 1024), v16(256, 1024), v16(128, 1024),
+        v16(512, 1024), v16(256, 1024), v16(128, 1024), v16(512, 1024), v16(1024, 512),
         v16(512, 2048), v16(256, 2048), v16(128, 2048), v16(64, 2048),
         v32(64, 2048), v32(64, 2048), v32(32, 2048), v32(32, 2048),
         v32(6, 16, 1024), v32(5, 16, 1024),
-        dma((36,)), dma((26,)), dma((26,)), dma((12, 5)), dma((12, 5)), dma((5,)), dma((5,)),
+        dma((36,)), dma((9,)), dma((9,)), dma((34,)), dma((34,)), dma((16, 5)), dma((16, 5)), dma((5,)), dma((5,)),
     ]
     shapes = [((TOK, D), BF16)] * 2 + [((2, TOK), F32), ((32, FF), F32), ((D, 128), F32)]
     shapes += [((32, D), F32)] * 4 + [((128,), F32)] + [((32,), F32)] * 5

time: 136 us -> 126 us (0.926)
  Pallas kernels: 135 us -> 125 us
    pallas_call x1, Pallas kernels: 132 us -> 122 us  [layer_on_device(): pl.pallas_call(layer_kernel, out_shape=shapes, in_specs=[pl.BlockSpec(mem...]
where the time goes in v4:
time: 126 us
  Pallas kernels  125 us (99%)
    pallas_call x1, Pallas kernels, layer_on_device(): pl.pallas_call(layer_kernel, out_shape=shapes, in_specs=[pl.BlockSpec(mem...  122 us
    pallas_call x1, Pallas kernels, layer_on_device(): pl.pallas_call(finish_kernel, out_shape=shapes, in_specs=[hbm] * 15, out_...  2.82 us

profile of v4, /device:TPU:0, one launch (start us, length us, event | category | flops | bytes accessed | tf_op | source)
XLA Modules:
  0.0 125.6 jit_solution(1844325566820944935)
XLA Ops:
  0.7 122.0 %shard_map.262 = (bf16[256,1024]{1,0:T(8,128)(2,1)}, bf16[256,1024]{1,0:T(8,128)(2,1)}, f32[2,256]{1,0:T(2,128)}, f32[32,4096]{1,0:T(8,128)}, f32[1024,128]{1,0:...) custom-call(s32[1,4]{1,0:T(1,128)} %doc.1, ...), custom_call_target="tpu_custom_call" | custom-call | tf_op jit(solution)/shard_map/pallas_call | solution.py:1097
  122.6 2.8 %shard_map.263 = (bf16[256,1024]{1,0:T(8,128)(2,1)}, bf16[256,1024]{1,0:T(8,128)(2,1)}, f32[2,256]{1,0:T(2,128)}, f32[32,4096]{1,0:T(8,128)}, f32[1024,128]{1,0:...) custom-call(bf16[256,1024]{1,0:T(8,128)(2,1)} %get-tuple-element.45., ...), custom_call_target="tpu_custom_call" | custom-call | tf_op jit(solution)/shard_map/pallas_call | solution.py:1115

commit v5 on v4

--- a/solution.py
+++ b/solution.py
@@ -328,43 +328,43 @@
 CHUNK = 128
 VMEM_BYTES = 62 * 1024 * 1024
 UNIT_ORDER = (
-    "wxyv",
+    "ywvx",
+    "wvxy",
     "ywxv",
     "yxwv",
-    "wyxv",
     "wyv",
     "ywv",
     "ywv",
     "ywv",
-    "ywxv",
+    "yxwv",
     "yxwv",
     "wxyv",
     "xywv",
+    "xywv",
     "xwyv",
     "xywv",
-    "yxwv",
-    "xywv",
+    "xwyv",
 )
 SLOTS = (
     (0, 1, 10, 11,),
     (),
     (),
-    (20, 30,),
+    (20,),
     (2, 12,),
     (),
     (21,),
     (),
     (3, 13,),
-    (22, 31, 80, 32,),
+    (30,),
+    (4, 22,),
     (),
-    (),
-    (100,),
-    (),
-    (14, 81, 23,),
-    (40, 82, 50, 33,),
-    (34, 102,),
-    (41, 51, 83, 160, 42, 4, 101, 84, 52, 43, 53, 24, 60, 103, 44, 15, 61, 5, 35, 54, 45, 70, 62, 104, 16, 110, 161, 111, 63, 85, 25, 6, 72, 120, 112, 105, 36, 71, 121, 113, 162, 64, 55, 90, 114, 130, 86, 122, 91, 73, 131, 26,),
-    (123, 74, 106, 140, 92, 132, 65, 163, 150, 93, 133, 115, 75, 141, 142, 94, 164, 151, 134, 116, 152, 124, 95, 143, 144, 135, 96, 153, 154, 136, 145, 125, 155, 146, 126, 156,),
+    (31,),
+    (110,),
+    (14, 100, 23,),
+    (40, 50, 111, 5, 32,),
+    (24, 112,),
+    (41, 33, 160, 102, 15, 101, 42, 52, 113, 6, 114, 51, 43, 16, 103, 60, 44, 34, 61, 115, 120, 53, 54, 25, 45, 70, 161, 62, 121, 35, 104, 116, 63, 130, 55, 122, 72, 131, 26, 123, 71, 162, 64, 105, 140, 36,),
+    (132, 80, 124, 141, 133, 81, 73, 150, 163, 74, 65, 106, 90, 142, 82, 134, 143, 125, 151, 83, 152, 164, 75, 92, 126, 84, 91, 144, 135, 153, 154, 85, 145, 93, 94, 136, 155, 86, 146, 95, 156, 96,),
 )
 
 
@@ -393,14 +393,26 @@
 def layer_kernel(
     doc, tok, cot, gain_a, gain_b, gain_c, gain_d, bias_up, bias_down,
     wq_hbm, wk_hbm, wv_hbm, wo_hbm, wu_hbm, wd_hbm,
-    out, grad_tok, rms, o_down, o_up, o_out, o_query, o_key, o_value,
-    small_up, small_down, small_a, small_b, small_c, small_d,
-    wq, wk, wv, wo, wu, wd, xin, q_t, k_t, v_t, k_n, v_n, mask, attn_t, attn_nat, attn_oth,
-    branch, hid, xm, act, g_t, part_send, part_recv, part_own, nat, gb_t, gba_t, ga_t,
-    rope, lse, stat, s_down, r1_down, r2_down, r3_down, r4_down, r1_up, r2_up, r3_up, xm_m, pre_m,
-    r1_late, r2_late, r3_late, r4_late, fin_down, fin_late, rec_down, rec_late, aux_s, aux_r,
-    w_sem, m_send, m_recv, c_send, c_recv, rs_send, rs_recv, a_send, a_recv,
+    *refs,
 ):
+    results, refs = refs[:15], refs[15:]
+    (
+        out, grad_tok, rms, o_down, o_up, o_out, o_query, o_key, o_value,
+        small_up, small_down, small_a, small_b, small_c, small_d, o_sem,
+        wq, wk, wv, wo, wu, wd, xin, q_t, k_t, v_t, k_n, v_n, mask, attn_t, attn_nat,
+        branch, hid, xm, act, g_t, part_send, part_recv, part_own, nat, gb_t,
+        rope, lse, stat, s_down, r1_down, r2_down, r3_down, r4_down, r1_up, r2_up, r3_up, xm_m, pre_m,
+        r1_late, r2_late, r3_late, r4_late, aux_s, aux_r,
+        w_sem, m_send, m_recv, c_send, c_recv, rs_send, rs_recv, a_send, a_recv,
+    ) = refs
+    held = (
+        out, grad_tok, rms, o_down, o_up, o_out, o_query, o_key, o_value,
+        small_up, small_down, small_a, small_b, small_c, small_d,
+    )
+
+    def hand_over(i):
+        return pltpu.make_async_copy(held[i], results[i], o_sem.at[i])
+
     dp = lax.axis_index("dp")
     b = lax.axis_index("blk")
     x = lax.rem(dp, 2)
@@ -434,14 +446,14 @@
         return pltpu.make_async_copy(
             wu_hbm.at[:, pl.ds(al((2 * j + b) * 128, 128), 128)],
             wu.at[:, pl.ds(al(j * 128, 128), 128)],
-            w_sem.at[4 + j],
+            w_sem.at[4],
         )
 
     def down_copy(j):
         return pltpu.make_async_copy(
             wd_hbm.at[pl.ds(al((2 * j + b) * 128, 128), 128)],
             wd.at[pl.ds(al(j * 128, 128), 128)],
-            w_sem.at[20 + j],
+            w_sem.at[5],
         )
 
     def to_core(k, src, dst):
@@ -449,20 +461,6 @@
             src_ref=src, dst_ref=dst, send_sem=c_send.at[k], recv_sem=c_recv.at[k],
             device_id=core_peer, device_id_type=MESH_ID,
         )
-
-    def pre_attn(i, carry):
-        rows = pl.ds(al(i * CHUNK, CHUNK), CHUNK)
-        v = tok[rows, :].astype(F32)
-        xin[pl.ds(al(own_tok + i * CHUNK, CHUNK), CHUNK), :] = (
-            v * inv_rms(v) * gain_a[...]
-        ).astype(BF16)
-        return carry
-
-    lax.fori_loop(0, TOK // CHUNK, pre_attn, 0)
-    pl.semaphore_wait(barrier, 5)
-    own_rows = xin.at[pl.ds(own_tok, TOK)]
-    xin_copy = to_core(0, own_rows, own_rows)
-    xin_copy.start()
 
     end_a = doc[0, 0]
     end_b = end_a + doc[0, 1]
@@ -486,10 +484,28 @@
         key_index = lax.broadcasted_iota(jnp.int32, (64, PACK), 0) + i * 64
         query_index = lax.broadcasted_iota(jnp.int32, (64, PACK), 1)
         allowed = (key_index <= query_index) & (key_index >= start_row)
-        mask[rows, :] = jnp.where(allowed, 0.0, neg_big)
+        mask[rows, :] = jnp.where(allowed, 0.0, neg_big).astype(BF16)
         return carry
 
     lax.fori_loop(0, 8, fill_mask, 0)
+
+    def pre_attn(i, carry):
+        rows = pl.ds(al(i * CHUNK, CHUNK), CHUNK)
+        v = tok[rows, :].astype(F32)
+        xin[pl.ds(al(own_tok + i * CHUNK, CHUNK), CHUNK), :] = (
+            v * inv_rms(v) * gain_a[...]
+        ).astype(BF16)
+        return carry
+
+    lax.fori_loop(0, TOK // CHUNK, pre_attn, 0)
+    pl.semaphore_wait(barrier, 5)
+    own_rows = xin.at[pl.ds(own_tok, TOK)]
+    xin_copy = to_core(0, own_rows, own_rows)
+    xin_copy.start()
+    lax.fori_loop(0, 16, lambda j, c: (up_copy(j).start(), c)[1], 0)
+    lax.fori_loop(0, 16, lambda j, c: (down_copy(j).start(), c)[1], 0)
+
+    attn_oth = nat.at[:, pl.ds(0, PACK)]
 
     def project(tok_at):
         rows = pl.ds(tok_at, TOK)
@@ -513,8 +529,6 @@
 
     for copy in w_copies[:3]:
         copy.wait()
-    lax.fori_loop(0, 16, lambda j, c: (up_copy(j).start(), c)[1], 0)
-    lax.fori_loop(0, 16, lambda j, c: (down_copy(j).start(), c)[1], 0)
     project(own_tok)
     xin_copy.wait()
     project(oth_tok)
@@ -532,7 +546,7 @@
             for w in (0, 1)
         ]
         scores = [
-            mm(k_n[:keys, slab_cols], slab(q_t[rows, cols], w)) + mask[:keys, cols]
+            mm(k_n[:keys, slab_cols], slab(q_t[rows, cols], w)) + mask[:keys, cols].astype(F32)
             for w, rows, cols, keys in parts
         ]
         tops = [jnp.max(score, axis=0, keepdims=True) for score in scores]
@@ -576,8 +590,8 @@
     xm_copy = to_core(5, own_rows_m, own_rows_m)
     xm_copy.start()
     xm_mate = pltpu.make_async_remote_copy(
-        src_ref=own_rows_m, dst_ref=xm_m.at[pl.ds(own_tok, TOK)], send_sem=m_send.at[8],
-        recv_sem=m_recv.at[8], device_id=x_peer, device_id_type=MESH_ID,
+        src_ref=own_rows_m, dst_ref=xm_m.at[pl.ds(own_tok, TOK)], send_sem=m_send.at[1],
+        recv_sem=m_recv.at[1], device_id=x_peer, device_id_type=MESH_ID,
     )
     xm_mate.start()
 
@@ -597,11 +611,11 @@
         )
         g_t[cols, rows] = slope.astype(BF16).T
 
-    lax.fori_loop(0, 16, lambda j, c: (up_copy(j).wait(), c)[1], 0)
+    pltpu.make_async_copy(wu_hbm.at[:, pl.ds(0, HALF_FF)], wu, w_sem.at[4]).wait()
     lax.fori_loop(0, 2, lambda i, c: (up_step(own_tok, i), c)[1], 0)
     xm_copy.wait()
     lax.fori_loop(0, 2, lambda i, c: (up_step(oth_tok, i), c)[1], 0)
-    lax.fori_loop(0, 16, lambda j, c: (down_copy(j).wait(), c)[1], 0)
+    pltpu.make_async_copy(wd_hbm.at[pl.ds(0, HALF_FF)], wd, w_sem.at[5]).wait()
 
     def down_step(tok_at, dst, i):
         cols = slice(i * 512, i * 512 + 512)
@@ -609,7 +623,7 @@
 
     mlp_copies = [
         to_core(k, part_send.at[:, pl.ds(i * 512, 512)], part_recv.at[:, pl.ds(i * 512, 512)])
-        for i, k in ((0, 6), (1, 31))
+        for i, k in ((0, 6), (1, 15))
     ]
     for i in range(2):
         down_step(oth_tok, part_send, i)
@@ -647,7 +661,7 @@
     zero_row = jnp.zeros((1, D), F32)
     sums = (zero_row, zero_row)
     gb_copies = []
-    for i, k in ((0, 7), (1, 32)):
+    for i, k in ((0, 7), (1, 16)):
         sums = post_mlp(i, sums)
         gb_copies.append(turn_and_send(gb_t, i, k))
     sum_bias_down, sum_gain_d = sums
@@ -656,6 +670,8 @@
     aux_s[0, 4:5, :] = sum_gain_d
     for i in range(2):
         rms[i : i + 1, :] = stat[i].T[0:1, :]
+    hand_over(0).start()
+    hand_over(2).start()
 
     for copy in gb_copies:
         copy.wait()
@@ -700,7 +716,7 @@
             src = refs[0].at[pl.ds(al(at, count), count), cols]
             dst = refs[k].at[:, cols]
         return pltpu.make_async_remote_copy(
-            src_ref=src, dst_ref=dst, send_sem=rs_send.at[n, k], recv_sem=rs_recv.at[n, k],
+            src_ref=src, dst_ref=dst, send_sem=rs_send.at[n], recv_sem=rs_recv.at[n, k],
             device_id=peer, device_id_type=MESH_ID,
         )
 
@@ -741,29 +757,42 @@
             if 4 <= n < 8:
                 o_up[c0 : c0 + width, :] = total.T
             else:
-                (fin_down if n < 4 else fin_late)[:, cols] = total
+                at, to = final_at(n)
+                part_own[at : at + 64, to : to + width] = total
                 final_copy(n).start()
 
-    oth_cut = pl.ds(al(other * 32, 32), 32)
-    own_cut = pl.ds(al(b * 32, 32), 32)
+    def final_at(n):
+        return (64 * n, 0) if n < 4 else (64 * ((n - 8) // 2), 512 + 256 * (n % 2))
+
+    def final_rows(n, half):
+        at, to = final_at(n)
+        return pl.ds(al(at + half * 32, 32), 32), pl.ds(to, units[n][2])
 
     def final_copy(n):
-        _, c0, width, _ = units[n]
-        cols = pl.ds(c0, width)
-        src, dst = (fin_down, rec_down) if n < 4 else (fin_late, rec_late)
-        return to_core(14 + n, src.at[oth_cut, cols], dst.at[:, cols])
+        at, to = (32 * n, 0) if n < 4 else (128 + 32 * ((n - 8) // 2), 256 * (n % 2))
+        dst = attn_t.at[pl.ds(at, 32), pl.ds(to, units[n][2])]
+        return final_with(part_own.at[final_rows(n, other)], dst, 18 if n < 4 else 19)
+
+    def final_with(src, dst, k):
+        return pltpu.make_async_remote_copy(
+            src_ref=src, dst_ref=dst, send_sem=c_send.at[18], recv_sem=c_recv.at[k],
+            device_id=core_peer, device_id_type=MESH_ID,
+        )
 
     aux_peers = (core_peer, x_peer, y_peer, z_low, z_high)
+
+    def aux_sum(k):
+        return aux_s.at[0] if k == 0 else hid.at[pl.ds(16 * k, 16)]
 
     def aux_copy(k):
         return pltpu.make_async_remote_copy(
-            src_ref=aux_s.at[k], dst_ref=aux_r.at[k], send_sem=a_send.at[k],
+            src_ref=aux_sum(k), dst_ref=aux_r.at[k], send_sem=a_send.at[k],
             recv_sem=a_recv.at[k], device_id=aux_peers[k], device_id_type=MESH_ID,
         )
 
     def aux_end(k):
         aux_copy(k).wait_recv()
-        aux_s[k + 1] = aux_s[k] + aux_r[k]
+        aux_sum(k + 1)[...] = aux_sum(k)[...] + aux_r[k]
         if k < 4:
             aux_copy(k + 1).start()
 
@@ -811,7 +840,7 @@
         return pltpu.make_async_remote_copy(
             src_ref=g_t.at[pl.ds(al((2 * k + 1 - x) * 128, 128), 128)],
             dst_ref=pre_m.at[pl.ds(al(k * 128, 128), 128)],
-            send_sem=m_send.at[k], recv_sem=m_recv.at[k],
+            send_sem=m_send.at[0], recv_sem=m_recv.at[0],
             device_id=x_peer, device_id_type=MESH_ID,
         )
 
@@ -823,10 +852,6 @@
         return carry
 
     lax.fori_loop(0, 4, act_back, 0)
-    xm_mate.wait()
-    mate_rows = xm_m.at[pl.ds(own_tok, TOK)]
-    xm_pass = to_core(30, mate_rows, mate_rows)
-    xm_pass.start()
     slot(2)
 
     def mlp_back(tok_at, dst, i):
@@ -837,6 +862,10 @@
     mlp_back_copy = to_core(8, part_send, part_recv)
     mlp_back_copy.start()
     slot(3)
+    xm_mate.wait()
+    mate_rows = xm_m.at[pl.ds(own_tok, TOK)]
+    xm_pass = to_core(14, mate_rows, mate_rows)
+    xm_pass.start()
     lax.fori_loop(0, 2, lambda i, c: (mlp_back(own_tok, part_own, i), c)[1], 0)
     ones = jnp.ones((16, PACK), BF16)
     for i in range(2):
@@ -844,6 +873,9 @@
     slot(4)
     mlp_back_copy.wait()
 
+    gba_t = wd.at[pl.ds(D, D), pl.ds(0, PACK)]
+    ga_t = wd.at[pl.ds(D, HALF_D), pl.ds(PACK, PACK)]
+
     def hidden_back(i, carry):
         sum_c, sum_b = carry
         rows = pl.ds(al(i * CHUNK, CHUNK), CHUNK)
@@ -860,7 +892,7 @@
 
     sums = (zero_row, zero_row)
     gba_copies = []
-    for i, k in ((0, 9), (1, 33)):
+    for i, k in ((0, 9), (1, 17)):
         sums = hidden_back(i, sums)
         gba_copies.append(turn_and_send(gba_t, i, k))
     sum_gain_c, sum_gain_b = sums
@@ -901,7 +933,7 @@
             for w, rows, cols, keys in parts
         ]
         scores = [
-            mm(k_n[:keys, slab_cols], slab(q_t[rows, cols], w)) + mask[:keys, cols]
+            mm(k_n[:keys, slab_cols], slab(q_t[rows, cols], w)) + mask[:keys, cols].astype(F32)
             for w, rows, cols, keys in parts
         ]
         g_probs = [
@@ -990,10 +1022,13 @@
         return carry + part_a
 
     aux_s[0, 1:2, :] = lax.fori_loop(0, TOK // CHUNK, token_back, zero_row)
+    hand_over(1).start()
     slot(14)
 
-    for k in range(8):
-        mate_copy(k).wait()
+    pltpu.make_async_remote_copy(
+        src_ref=pre_m, dst_ref=pre_m, send_sem=m_send.at[0], recv_sem=m_recv.at[0],
+        device_id=x_peer, device_id_type=MESH_ID,
+    ).wait()
     xm_pass.wait()
 
     def mate_pre(chip):
@@ -1009,47 +1044,59 @@
 
     aux_copy(0).start()
     slot(17)
-    for n in range(4):
-        final_copy(n).wait()
-
-    def place_down(j, carry):
-        from_cols = pl.ds(al(j * 128, 128), 128)
-        o_down[:, pl.ds(al((2 * j + b) * 128, 128), 128)] = fin_down[own_cut, from_cols]
-        o_down[:, pl.ds(al((2 * j + other) * 128, 128), 128)] = rec_down[:, from_cols]
-        return carry
-
-    lax.fori_loop(0, 16, place_down, 0)
+    finals = attn_t.at[pl.ds(0, 128)]
+    final_with(finals, finals, 18).wait_recv()
+
+    for j in range(16):
+        rows, _ = final_rows(j // 4, b)
+        at = j % 4 * 128
+        o_down[:, pl.ds(al((2 * j + b) * 128, 128), 128)] = part_own[rows, at : at + 128]
+        o_down[:, pl.ds(al((2 * j + other) * 128, 128), 128)] = attn_t[
+            j // 4 * 32 : j // 4 * 32 + 32, at : at + 128
+        ]
+    hand_over(3).start()
     slot(18)
+    hand_over(4).start()
     device = dp * 2 + b
     at = pl.ds(al(device // 4 * 128, 128), 128)
-    lines = pltpu.roll(aux_s[5, 0:8, at], lax.rem(128 - lax.rem(device, 4) * 32, 128), 1)
+    lines = pltpu.roll(aux_sum(5)[0:8, at], lax.rem(128 - lax.rem(device, 4) * 32, 128), 1)
     for i, ref in enumerate((small_down, small_a, small_b, small_c, small_d)):
         ref[...] = lines[i, :32]
-    lines = aux_s[5, 8:16, pl.ds(al(lax.rem(dp, 8) * 128, 128), 128)]
+    lines = aux_sum(5)[8:16, pl.ds(al(lax.rem(dp, 8) * 128, 128), 128)]
     chosen = lax.broadcasted_iota(jnp.int32, (8, 128), 0) == 2 * b + dp // 8
     small_up[...] = jnp.sum(jnp.where(chosen, lines, 0.0), axis=0)
-    for n in range(len(units)):
-        for k in range(len(UNIT_ORDER[n]) + 1):
-            unit_copy(n, k).wait_send()
+    for i in range(9, 15):
+        hand_over(i).start()
+    for n, (refs, c0, width, rows) in enumerate(units):
+        sent = refs[0].at[pl.ds(0, (2 ** len(UNIT_ORDER[n]) - 1) * rows), pl.ds(c0, width)]
+        pltpu.make_async_remote_copy(
+            src_ref=sent, dst_ref=sent, send_sem=rs_send.at[n], recv_sem=rs_recv.at[n, 0],
+            device_id=x_peer, device_id_type=MESH_ID,
+        ).wait_send()
     for k in range(5):
         aux_copy(k).wait_send()
+    whole = part_own.at[pl.ds(0, 128)]
+    final_with(whole, whole, 18).wait_send()
+    finals = attn_t.at[pl.ds(128, 128)]
+    final_with(finals, finals, 19).wait_recv()
     for i in range(4):
-        final_copy(8 + 2 * i).wait()
-        final_copy(9 + 2 * i).wait()
-        cols = slice(i * 512, i * 512 + 512)
         dst = (o_out, o_query, o_key, o_value)[i]
-        dst[:, pl.ds(own_cols, HALF_D)] = fin_late[own_cut, cols]
-        dst[:, pl.ds(oth_cols, HALF_D)] = rec_late[:, cols]
+        rows, _ = final_rows(8 + 2 * i, b)
+        dst[:, pl.ds(own_cols, HALF_D)] = part_own[rows, 512:]
+        dst[:, pl.ds(oth_cols, HALF_D)] = attn_t[128 + 32 * i : 160 + 32 * i, :]
+        hand_over(5 + i).start()
+    for i in range(15):
+        hand_over(i).wait()
 
 
 def finish_kernel(*refs):
     count = len(refs) // 3
     sems = refs[-1]
     gets = [
-        pltpu.make_async_copy(refs[i], refs[2 * count + i], sems.at[0, i]) for i in range(count)
+        pltpu.make_async_copy(refs[i], refs[2 * count + i], sems.at[i]) for i in range(count)
     ]
     puts = [
-        pltpu.make_async_copy(refs[2 * count + i], refs[count + i], sems.at[1, i])
+        pltpu.make_async_copy(refs[2 * count + i], refs[count + i], sems.at[i])
         for i in range(count)
     ]
     for copy in gets:
@@ -1073,34 +1120,35 @@
 
     dma = pltpu.SemaphoreType.DMA
     vmem = pl.BlockSpec(memory_space=pltpu.VMEM)
-    scratch = [
+    hbm = pl.BlockSpec(memory_space=pltpu.HBM)
+    shapes = [((TOK, D), BF16)] * 2 + [((2, TOK), F32), ((32, FF), F32), ((D, 128), F32)]
+    shapes += [((32, D), F32)] * 4 + [((128,), F32)] + [((32,), F32)] * 5
+    shapes = [jax.ShapeDtypeStruct(*shape) for shape in shapes]
+    scratch = [pltpu.VMEM(shape.shape, shape.dtype) for shape in shapes] + [dma((15,))]
+    scratch += [
         v16(1024, 512), v16(1024, 512), v16(1024, 512), v16(1024, 1024),
         v16(1024, 2048), v16(2048, 1024),
         v16(512, 1024),
         v16(512, 512), v16(512, 512), v16(512, 512), v16(512, 512), v16(512, 512),
-        v32(512, 512), v32(512, 512), v16(512, 512), v16(256, 512),
+        v16(512, 512), v32(512, 512), v16(512, 512),
         v32(256, 1024), v32(256, 1024), v16(512, 1024),
         v16(512, 2048), v16(2048, 512),
         v16(256, 1024), v16(256, 1024), v32(256, 1024), v16(256, 1024),
-        v16(1024, 512), v16(1024, 512), v16(512, 512),
+        v16(1024, 512),
         v32(2, 32, 512), v32(8, 512), v32(2, 256, 128),
         v16(1024, 2048), v16(512, 2048), v16(256, 2048), v16(128, 2048), v16(64, 2048),
         v16(512, 1024), v16(256, 1024), v16(128, 1024), v16(512, 1024), v16(1024, 512),
         v16(512, 2048), v16(256, 2048), v16(128, 2048), v16(64, 2048),
-        v32(64, 2048), v32(64, 2048), v32(32, 2048), v32(32, 2048),
-        v32(6, 16, 1024), v32(5, 16, 1024),
-        dma((36,)), dma((9,)), dma((9,)), dma((34,)), dma((34,)), dma((16, 5)), dma((16, 5)), dma((5,)), dma((5,)),
+        v32(1, 16, 1024), v32(5, 16, 1024),
+        dma((6,)), dma((2,)), dma((2,)), dma((20,)), dma((20,)), dma((16,)), dma((16, 5)), dma((5,)), dma((5,)),
     ]
-    shapes = [((TOK, D), BF16)] * 2 + [((2, TOK), F32), ((32, FF), F32), ((D, 128), F32)]
-    shapes += [((32, D), F32)] * 4 + [((128,), F32)] + [((32,), F32)] * 5
-    shapes = [jax.ShapeDtypeStruct(*shape) for shape in shapes]
     results = pl.pallas_call(
         layer_kernel,
         out_shape=shapes,
         in_specs=[pl.BlockSpec(memory_space=pltpu.SMEM)]
         + [vmem] * 8
         + [pl.BlockSpec(memory_space=pl.ANY)] * 6,
-        out_specs=[vmem] * 15,
+        out_specs=[hbm] * 15,
         scratch_shapes=scratch,
         compiler_params=pltpu.CompilerParams(
             collective_id=0, has_side_effects=True, vmem_limit_bytes=VMEM_BYTES
@@ -1111,13 +1159,12 @@
         bias_up.reshape(32, 128), bias_down[None],
         w_query, w_key, w_value, w_out, w_up, w_down,
     )
-    hbm = pl.BlockSpec(memory_space=pltpu.HBM)
     out, grad_tok, rms, gd, gu, go, gq, gk, gv, small_up, small_down, sa, sb, sc, sd = pl.pallas_call(
         finish_kernel,
         out_shape=shapes,
         in_specs=[hbm] * 15,
         out_specs=[hbm] * 15,
-        scratch_shapes=[pltpu.VMEM(s.shape, s.dtype) for s in shapes] + [dma((2, 15))],
+        scratch_shapes=[pltpu.VMEM(s.shape, s.dtype) for s in shapes] + [dma((15,))],
     )(*results)
     return (
         out, grad_tok, gq.T, gk.T, gv.T, go.T, gu, gd.T, small_up, small_down, sa, sb, sc, sd, rms

time: 126 us -> 122 us (0.968)
  Pallas kernels: 125 us -> 121 us
    pallas_call x1, Pallas kernels: 122 us -> 119 us  [layer_on_device(): pl.pallas_call(layer_kernel, out_shape=shapes, in_specs=[pl.BlockSpec(mem...]
where the time goes in v5:
time: 122 us
  Pallas kernels  121 us (99%)
    pallas_call x1, Pallas kernels, layer_on_device(): pl.pallas_call(layer_kernel, out_shape=shapes, in_specs=[pl.BlockSpec(mem...  119 us
    pallas_call x1, Pallas kernels, layer_on_device(): pl.pallas_call(finish_kernel, out_shape=shapes, in_specs=[hbm] * 15, out_...  2.69 us

profile of v5, /device:TPU:0, one launch (start us, length us, event | category | flops | bytes accessed | tf_op | source)
XLA Modules:
  0.0 122.3 jit_solution(14780064388461359031)
XLA Ops:
  0.7 118.8 %shard_map.262 = (bf16[256,1024]{1,0:T(8,128)(2,1)}, bf16[256,1024]{1,0:T(8,128)(2,1)}, f32[2,256]{1,0:T(2,128)}, f32[32,4096]{1,0:T(8,128)}, f32[1024,128]{1,0:...) custom-call(s32[1,4]{1,0:T(1,128)} %doc.1, ...), custom_call_target="tpu_custom_call" | custom-call | tf_op jit(solution)/shard_map/pallas_call | solution.py:1145
  119.4 2.7 %shard_map.263 = (bf16[256,1024]{1,0:T(8,128)(2,1)}, bf16[256,1024]{1,0:T(8,128)(2,1)}, f32[2,256]{1,0:T(2,128)}, f32[32,4096]{1,0:T(8,128)}, f32[1024,128]{1,0:...) custom-call(bf16[256,1024]{1,0:T(8,128)(2,1)} %get-tuple-element.45., ...), custom_call_target="tpu_custom_call" | custom-call | tf_op jit(solution)/shard_map/pallas_call | solution.py:1162

commit v6 on v5

--- a/solution.py
+++ b/solution.py
@@ -484,7 +484,7 @@
         key_index = lax.broadcasted_iota(jnp.int32, (64, PACK), 0) + i * 64
         query_index = lax.broadcasted_iota(jnp.int32, (64, PACK), 1)
         allowed = (key_index <= query_index) & (key_index >= start_row)
-        mask[rows, :] = jnp.where(allowed, 0.0, neg_big).astype(BF16)
+        mask[rows, :] = jnp.where(allowed, 0.0, neg_big)
         return carry
 
     lax.fori_loop(0, 8, fill_mask, 0)
@@ -538,30 +538,36 @@
     def slab(head_rows, which):
         return jnp.concatenate([head_rows, zeros] if which == 0 else [zeros, head_rows], axis=0)
 
-    def attend(p, carry):
-        slab_cols = pl.ds(al(p * 128, 128), 128)
+    def attend(i, carry):
+        pairs = [2 * i, 2 * i + 1]
+        slabs = [pl.ds(al(p * 128, 128), 128) for p in pairs]
         parts = [
-            (w, pl.ds(al(p * 128 + w * 64, 64), 64), slice(i * TOK, i * TOK + TOK), (i + 1) * TOK)
-            for i in (1, 0)
+            (
+                w, pl.ds(al(pairs[e] * 128 + w * 64, 64), 64),
+                slice(block * TOK, block * TOK + TOK), (block + 1) * TOK, e,
+            )
+            for e in (0, 1)
+            for block in (1, 0)
             for w in (0, 1)
         ]
         scores = [
-            mm(k_n[:keys, slab_cols], slab(q_t[rows, cols], w)) + mask[:keys, cols].astype(F32)
-            for w, rows, cols, keys in parts
+            mm(k_n[:keys, slabs[e]], slab(q_t[rows, cols], w)) + mask[:keys, cols]
+            for w, rows, cols, keys, e in parts
         ]
         tops = [jnp.max(score, axis=0, keepdims=True) for score in scores]
         weights = [jnp.exp(score - top) for score, top in zip(scores, tops)]
         totals = [jnp.sum(weight, axis=0, keepdims=True) for weight in weights]
-        for (w, rows, cols, keys), weight, top, total in zip(parts, weights, tops, totals):
+        for (w, rows, cols, keys, e), weight, top, total in zip(parts, weights, tops, totals):
             attn_t[rows, cols] = mm(v_t[rows, :keys], weight.astype(BF16)) * (1.0 / total)
-            lse[pl.ds(p * 2 + w, 1), cols] = top + jnp.log(total)
-        attn_nat[:, slab_cols] = attn_t[pl.ds(al(p * 128, 128), 128), :].T.astype(BF16)
-        to_core(
-            1 + p, attn_nat.at[pl.ds(oth_tok, TOK), slab_cols], attn_oth.at[:, slab_cols]
-        ).start()
+            lse[pl.ds(pairs[e] * 2 + w, 1), cols] = top + jnp.log(total)
+        for p, slab_cols in zip(pairs, slabs):
+            attn_nat[:, slab_cols] = attn_t[pl.ds(al(p * 128, 128), 128), :].T.astype(BF16)
+            to_core(
+                1 + p, attn_nat.at[pl.ds(oth_tok, TOK), slab_cols], attn_oth.at[:, slab_cols]
+            ).start()
         return carry
 
-    lax.fori_loop(0, 4, attend, 0)
+    lax.fori_loop(0, 2, attend, 0)
 
     w_copies[3].wait()
     branch[...] = mm(attn_nat[pl.ds(own_tok, TOK), :], wo[pl.ds(own_cols, HALF_D), :])
@@ -933,7 +939,7 @@
             for w, rows, cols, keys in parts
         ]
         scores = [
-            mm(k_n[:keys, slab_cols], slab(q_t[rows, cols], w)) + mask[:keys, cols].astype(F32)
+            mm(k_n[:keys, slab_cols], slab(q_t[rows, cols], w)) + mask[:keys, cols]
             for w, rows, cols, keys in parts
         ]
         g_probs = [
@@ -1130,7 +1136,7 @@
         v16(1024, 2048), v16(2048, 1024),
         v16(512, 1024),
         v16(512, 512), v16(512, 512), v16(512, 512), v16(512, 512), v16(512, 512),
-        v16(512, 512), v32(512, 512), v16(512, 512),
+        v32(512, 512), v32(512, 512), v16(512, 512),
         v32(256, 1024), v32(256, 1024), v16(512, 1024),
         v16(512, 2048), v16(2048, 512),
         v16(256, 1024), v16(256, 1024), v32(256, 1024), v16(256, 1024),

time: 122 us -> 122 us (level)
  no operation moved by 1% of the time
where the time goes in v6:
time: 122 us
  Pallas kernels  121 us (99%)
    pallas_call x1, Pallas kernels, layer_on_device(): pl.pallas_call(layer_kernel, out_shape=shapes, in_specs=[pl.BlockSpec(mem...  118 us
    pallas_call x1, Pallas kernels, layer_on_device(): pl.pallas_call(finish_kernel, out_shape=shapes, in_specs=[hbm] * 15, out_...  2.69 us

profile of v6, /device:TPU:0, one launch (start us, length us, event | category | flops | bytes accessed | tf_op | source)
XLA Modules:
  0.0 121.8 jit_solution(9664449435353769027)
XLA Ops:
  0.7 118.3 %shard_map.262 = (bf16[256,1024]{1,0:T(8,128)(2,1)}, bf16[256,1024]{1,0:T(8,128)(2,1)}, f32[2,256]{1,0:T(2,128)}, f32[32,4096]{1,0:T(8,128)}, f32[1024,128]{1,0:...) custom-call(s32[1,4]{1,0:T(1,128)} %doc.1, ...), custom_call_target="tpu_custom_call" | custom-call | tf_op jit(solution)/shard_map/pallas_call | solution.py:1151
  118.9 2.7 %shard_map.263 = (bf16[256,1024]{1,0:T(8,128)(2,1)}, bf16[256,1024]{1,0:T(8,128)(2,1)}, f32[2,256]{1,0:T(2,128)}, f32[32,4096]{1,0:T(8,128)}, f32[1024,128]{1,0:...) custom-call(bf16[256,1024]{1,0:T(8,128)(2,1)} %get-tuple-element.45., ...), custom_call_target="tpu_custom_call" | custom-call | tf_op jit(solution)/shard_map/pallas_call | solution.py:1168

commit v7 on v6

--- a/solution.py
+++ b/solution.py
@@ -802,9 +802,11 @@
         if k < 4:
             aux_copy(k + 1).start()
 
-    def slot(i):
+    def slot(i, only=None):
         for code in SLOTS[i]:
             n, k = code // 10, code % 10
+            if only is not None and n != only:
+                continue
             if n == len(units):
                 aux_end(k)
             elif k < 2:
@@ -840,7 +842,9 @@
             weight_grad(
                 n, first, first + 2, (rows_of(gb_t, 64), act[:, 512 * n : 512 * n + 512])
             )
-        slot(first // 2)
+            if first == 0:
+                slot(0, n)
+    slot(1)
 
     def mate_copy(k):
         return pltpu.make_async_remote_copy(

time: 122 us -> 122 us (level)
  no operation moved by 1% of the time
where the time goes in v7:
time: 122 us; the launch traced here: 121 us
  Pallas kernels  121 us (99%)
    pallas_call x1, Pallas kernels, layer_on_device(): pl.pallas_call(layer_kernel, out_shape=shapes, in_specs=[pl.BlockSpec(mem...  118 us
    pallas_call x1, Pallas kernels, layer_on_device(): pl.pallas_call(finish_kernel, out_shape=shapes, in_specs=[hbm] * 15, out_...  2.69 us

profile of v7, /device:TPU:0, one launch (start us, length us, event | category | flops | bytes accessed | tf_op | source)
XLA Modules:
  0.0 121.4 jit_solution(15174751428090988585)
XLA Ops:
  0.7 117.9 %shard_map.262 = (bf16[256,1024]{1,0:T(8,128)(2,1)}, bf16[256,1024]{1,0:T(8,128)(2,1)}, f32[2,256]{1,0:T(2,128)}, f32[32,4096]{1,0:T(8,128)}, f32[1024,128]{1,0:...) custom-call(s32[1,4]{1,0:T(1,128)} %doc.1, ...), custom_call_target="tpu_custom_call" | custom-call | tf_op jit(solution)/shard_map/pallas_call | solution.py:1155
  118.6 2.7 %shard_map.263 = (bf16[256,1024]{1,0:T(8,128)(2,1)}, bf16[256,1024]{1,0:T(8,128)(2,1)}, f32[2,256]{1,0:T(2,128)}, f32[32,4096]{1,0:T(8,128)}, f32[1024,128]{1,0:...) custom-call(bf16[256,1024]{1,0:T(8,128)(2,1)} %get-tuple-element.45., ...), custom_call_target="tpu_custom_call" | custom-call | tf_op jit(solution)/shard_map/pallas_call | solution.py:1172
